TPU v7x, 512 devices: a whole 4x8x8 slice. The times are simulated.
512 devices in a mesh: space: 64 (over z_lo, y, core), filt: 8 (over x, z_hi).
Axes of the slice: x: 4, y: 8, z: 8 (z_hi: 2, z_lo: 4; z = z_hi * 4 + z_lo), core: 2. Of those that a mesh axis runs over, the one named last changes fastest.
Arguments:
- activations: bfloat16 [256, 131072], P(None, 'space'), may hold values from -6 to 6
- out_grad: bfloat16 [256, 131072], P('filt', 'space'), may hold values from -6 to 6
- kernel: bfloat16 [256, 3, 3, 256], P('filt'), may hold values from -0.125 to 0.125
Outputs:
- input_grad: bfloat16 [256, 131072], P('filt', 'space')
- weight_grad: float32 [256, 3, 3, 256], P('filt')
All inputs are finite; a program needn't handle non-finite values.
Results may differ from a plain program's by a relative error of at most 0.015.
Values may be sent and summed in bfloat16 or wider, within the bound.
No kernel may reach another device: no remote copies, remote signals or barrier semaphores. Data moves between devices by JAX's collectives and lax.ppermute only.
A program may use at most 64 MiB of HBM per device.

v0:
```python
import math

import jax
import jax.numpy as jnp
from jax import lax
from jax.sharding import PartitionSpec as P

COLS = 1024


tap_offsets = [(-1, -1), (-1, 0), (-1, 1), (0, -1), (0, 0), (0, 1), (1, -1), (1, 0), (1, 1)]


def with_halo(array, sides, width):
    for axis, dim in sides:
        size, length = (lax.axis_size(axis), array.shape[dim])
        up = [(i, (i + 1) % size) for i in range(size - 1)]
        down = [(j, i) for i, j in up]
        last = lax.slice_in_dim(array, length - width, length, axis=dim)
        first = lax.slice_in_dim(array, 0, width, axis=dim)
        before = lax.ppermute(last, axis, up)
        after = lax.ppermute(first, axis, down)
        array = jnp.concatenate([before, array, after], axis=dim)
    return array


def widen(field):
    return jnp.pad(field, [(0, 0)] * (field.ndim - 1) + [(1, 1)])


def shifted(padded, row_step, col_step, columns, pixels):
    start = 1 + columns + row_step * columns + col_step
    window = lax.slice_in_dim(padded, start, start + pixels, axis=padded.ndim - 1)
    column = lax.broadcasted_iota(jnp.int32, (pixels,), 0) % columns + col_step
    inside = (column >= 0) & (column < columns)
    return jnp.where(inside, window, jnp.zeros((), window.dtype))


def body(activations, out_grad, kernel):
    channels = activations.shape[0]
    pixels = activations.shape[1]
    local_filters = out_grad.shape[0]
    contract_rows = (((1,), (1,)), ((), ()))
    grad_halo = with_halo(out_grad, (("space", 1),), COLS)
    grad_padded = widen(grad_halo)
    blocks = []
    input_padded = widen(with_halo(activations, (("space", 1),), COLS))
    for row_step, col_step in tap_offsets:
        moved = shifted(input_padded, row_step, col_step, COLS, pixels)
        blocks.append(
            lax.dot_general(out_grad, moved, contract_rows, preferred_element_type=jnp.float32)
        )
    scale = 1.0 / math.sqrt(pixels * lax.axis_size("space"))
    weight_local = jnp.stack(blocks, 1).reshape(local_filters, 3, 3, channels) * scale
    weight_grad = lax.psum(weight_local, "space")
    partial_value = jnp.zeros((channels, pixels), jnp.float32)
    for row_step, col_step in tap_offsets:
        back = shifted(grad_padded, -row_step, -col_step, COLS, pixels)
        taps = kernel[:, row_step + 1, col_step + 1, :]
        partial_value = partial_value + lax.dot_general(
            taps, back, (((0,), (0,)), ((), ())), preferred_element_type=jnp.float32
        )
    input_grad = lax.psum_scatter(
        partial_value.astype(jnp.bfloat16), "filt", scatter_dimension=0, tiled=True
    )
    return (input_grad, weight_grad)


def solution(mesh):
    in_specs = (P(None, "space"), P("filt", "space"), P("filt", None, None, None))
    out_specs = (P("filt", "space"), P("filt", None, None, None))
    return jax.shard_map(body, mesh=mesh, in_specs=in_specs, out_specs=out_specs, check_vma=False)
```

profile of v0, /device:TPU:1, one launch (start us, length us, event | category | flops | bytes accessed | tf_op | source)
XLA Modules:
  0.0 550.1 jit_solution(13166956920843262232)
XLA Ops:
  8.1 0.9 fusion.117
  9.0 4.6 collective-permute-start
  13.6 5.5 collective-permute-start.1
  19.1 1.3 fusion.116
  20.4 1.9 collective-permute-start.2
  22.3 2.4 collective-permute-start.3
  25.5 0.7 fusion.45
  26.2 0.7 fusion.44
  27.3 0.7 fusion.2
  28.0 0.7 convolution_add_fusion.3
  28.7 0.7 convolution_add_fusion.2
  29.9 0.7 copy-done
  30.8 2.0 collective-permute-done.3
  32.8 1.3 fusion.9
  35.0 0.6 fusion.16
  35.6 0.6 fusion.15
  36.6 0.6 fusion.13
  37.2 0.6 fusion.12
  38.1 0.6 fusion.10
  38.7 0.7 broadcast_multiply_fusion
  39.5 1.2 fusion.7
  40.8 1.4 copy.7
  42.2 498.7 %all-reduce.4.cloned.1.call-done = f32[32,3,3,256]{3,0,2,1:T(8,128)} async-done(((f32[32,3,3,256]{3,0,2,1:T(8,128)}), f32[32,3,3,256]{3,0,2,1:T(8,128)}) %all-reduce.4.cloned.1.call-update) | async-done | bytes 294928 | tf_op jit(solution)/shard_map/psum | solution.py:55
  540.9 1.7 copy.22
  (30 shorter events, 3.8 us)
Async XLA Ops:
  8.0 16.8 %copy-start.1 = (bf16[32,2048]{1,0:T(8,128)(2,1)S(1)}, bf16[32,2048]{1,0:T(8,128)(2,1)}, u32[]{:S(2)}) copy-start(bf16[32,2048]{1,0:T(8,128)(2,1)} %param.4) | copy-start | bytes 393220
  8.0 16.8 %copy-start.2 = (bf16[32,3,3,256]{3,0,2,1:T(8,128)(2,1)S(1)}, bf16[32,3,3,256]{3,0,2,1:T(8,128)(2,1)}, u32[]{:S(2)}) copy-start(bf16[32,3,3,256]{3,0,2,1:T(8,128)(2,1)} %param.5) | copy-start | bytes 442372
  8.0 532.9 %all-reduce.4.cloned.1.call-start = ((), (), s32[]{:S(2)}) async-start(), calls=%async_computation.1 | async-start | bytes 589824 | tf_op jit(solution)/shard_map/psum | solution.py:55
  9.0 16.3 %collective-permute-start = (bf16[32,1024]{1,0:T(8,128)(2,1)S(1)}, bf16[32,1024]{1,0:T(8,128)(2,1)S(1)}, u32[]{:S(2)}, u32[]{:S(2)}) collective-permute-start(bf16[32,1024]{1,0:T(8,128)(2,1)S(1)} %get-tuple-element.12), channel_id=1, source_target_pairs={{0,8},{8,16},{16,24},{24,32},{32,40},{40,48},{48,56},{56,64},{64,7... | collective-permute-start | bytes 196616 | tf_op jit(solution)/shard_map/ppermute | solution.py:21
  13.6 11.7 %collective-permute-start.1 = (bf16[32,1024]{1,0:T(8,128)(2,1)S(1)}, bf16[32,1024]{1,0:T(8,128)(2,1)S(1)}, u32[]{:S(2)}, u32[]{:S(2)}) collective-permute-start(bf16[32,1024]{1,0:T(8,128)(2,1)S(1)} %get-tuple-element.13), channel_id=1, source_target_pairs={{8,0},{16,8},{24,16},{32,24},{40,32},{48,40},{56,48},{64,56},{72,6... | collective-permute-start | bytes 196616 | tf_op jit(solution)/shard_map/ppermute | solution.py:22
  20.4 9.4 %collective-permute-start.2 = (bf16[256,1024]{1,0:T(8,128)(2,1)S(1)}, bf16[256,1024]{1,0:T(8,128)(2,1)S(1)}, u32[]{:S(2)}, u32[]{:S(2)}) collective-permute-start(bf16[256,1024]{1,0:T(8,128)(2,1)S(1)} %get-tuple-element.8), channel_id=1, source_target_pairs={{0,8},{8,16},{16,24},{24,32},{32,40},{40,48},{48,56},{56,64},{64,7... | collective-permute-start | bytes 1572872 | tf_op jit(solution)/shard_map/ppermute | solution.py:21
  22.3 10.5 %collective-permute-start.3 = (bf16[256,1024]{1,0:T(8,128)(2,1)S(1)}, bf16[256,1024]{1,0:T(8,128)(2,1)S(1)}, u32[]{:S(2)}, u32[]{:S(2)}) collective-permute-start(bf16[256,1024]{1,0:T(8,128)(2,1)S(1)} %get-tuple-element.9), channel_id=1, source_target_pairs={{8,0},{16,8},{24,16},{32,24},{40,32},{48,40},{56,48},{64,56},{72,6... | collective-permute-start | bytes 1572872 | tf_op jit(solution)/shard_map/ppermute | solution.py:22
  29.3 1.2 copy-start
  39.5 501.4 %reduce-scatter.4.cloned.1.call-start = ((), (), s32[]{:S(2)}) async-start(), calls=%async_computation.2 | async-start | bytes 1179648
Sparse Core Ops, SparseCore 0:
  39.6 501.2 all-reduce.3
Sparse Core Ops, SparseCore 1:
  45.0 94.9 reduce-scatter.3
where the time goes:
time: 551 us; the launch traced here: 550 us
  waiting for transfers between devices  501 us (91%)
  between operations  15.7 us (3%)
  starting transfers between devices  14.5 us (3%)
  matrix products  10.4 us (2%)
  local copies, waits for them, and re-layouts  6.38 us (1%)
    psum x1, waiting for transfers between devices, body(): weight_grad = lax.psum(weight_local, 'space')  499 us
  transfers between devices with their start and end apart: 6, of which 2 were waited for; matrix products, arithmetic and copies ran while one was open for 2% of the time, Pallas kernels for 0%

commit v1 on v0

v1 whole, which is shorter than its diff:
```python
import math

import jax
import jax.numpy as jnp
from jax import lax
from jax.sharding import PartitionSpec as P

COLS = 1024


def halo_rows(array):
    size = lax.axis_size("space")
    up = [(i, i + 1) for i in range(size - 1)]
    down = [(j, i) for i, j in up]
    before = lax.ppermute(array[:, -COLS:], "space", up)
    after = lax.ppermute(array[:, :COLS], "space", down)
    return before, after


def shifted_stack(out_grad, before, after):
    filters, pixels = out_grad.shape
    rows = jnp.concatenate([before, out_grad, after], axis=1)
    column = lax.broadcasted_iota(jnp.int32, (1, rows.shape[1]), 1) % COLS
    zero = jnp.zeros((), rows.dtype)
    right = jnp.where(column == 0, zero, jnp.roll(rows, 1, axis=1))
    left = jnp.where(column == COLS - 1, zero, jnp.roll(rows, -1, axis=1))
    by_col = {-1: right, 0: rows, 1: left}
    stack = []
    for i in range(3):
        for j in range(3):
            start = COLS * (2 - i)
            stack.append(by_col[1 - j][:, start:start + pixels])
    return jnp.concatenate(stack, axis=0)


def body(activations, out_grad, kernel):
    channels, pixels = activations.shape
    filters = out_grad.shape[0]
    n_space = lax.axis_size("space")
    n_filt = lax.axis_size("filt")
    scale = 1.0 / math.sqrt(pixels * n_space)
    before, after = halo_rows(out_grad)
    stack = shifted_stack(out_grad, before, after)
    terms = lax.dot_general(stack, activations, (((1,), (1,)), ((), ())), preferred_element_type=jnp.float32)
    terms = (terms * scale).astype(jnp.bfloat16)
    tiles = terms.reshape(36, 8, 2, 128).transpose(0, 2, 1, 3).reshape(72, 8, 128)
    low = tiles[:64]
    high = jnp.pad(tiles[64:], ((0, 56), (0, 0), (0, 0)))
    chunks = jnp.concatenate([low, high], axis=1)
    got = lax.all_to_all(chunks, "space", 0, 0, tiled=True)
    total = jnp.sum(got.astype(jnp.float32), axis=0).astype(jnp.bfloat16)
    everyone = jnp.broadcast_to(total[None], (n_space,) + total.shape)
    full = lax.all_to_all(everyone, "space", 0, 0, tiled=True)
    full = jnp.concatenate([full[:, :8], full[:8, 8:]], axis=0).astype(jnp.float32)
    weight = full.reshape(36, 2, 8, 128).transpose(0, 2, 1, 3).reshape(3, 3, filters, channels)
    weight_grad = weight.transpose(2, 0, 1, 3)

    taps = kernel.transpose(1, 2, 0, 3).reshape(9 * filters, channels)
    partial = lax.dot_general(taps, stack, (((0,), (0,)), ((), ())), preferred_element_type=jnp.float32)
    partial = partial.astype(jnp.bfloat16)
    shares = lax.all_to_all(partial, "filt", 0, 0, tiled=True).reshape(n_filt, channels // n_filt, pixels)
    input_grad = jnp.sum(shares.astype(jnp.float32), axis=0).astype(jnp.bfloat16)
    return (input_grad, weight_grad)


def solution(mesh):
    in_specs = (P(None, "space"), P("filt", "space"), P("filt", None, None, None))
    out_specs = (P("filt", "space"), P("filt", None, None, None))
    return jax.shard_map(body, mesh=mesh, in_specs=in_specs, out_specs=out_specs, check_vma=False)
```

time: 551 us -> 98 us (0.18)
  the two profiles are of different devices: /device:TPU:1 before, /device:TPU:64 now
where the time goes in v1:
time: 98 us; the launch traced here: 97.6 us
  waiting for transfers between devices  45.9 us (47%)
  starting transfers between devices  22.1 us (23%)
  blocking collectives  21.2 us (22%)
  local copies, waits for them, and re-layouts  3.45 us (4%)
  matrix products  2.23 us (2%)
  other arithmetic  1.88 us (2%)
    all_to_all x1, waiting for transfers between devices, body(): lax.all_to_all(partial, 'filt', 0, 0, tiled=True)  30.4 us
    all_to_all x1, blocking collectives, body(): got = lax.all_to_all(chunks, 'space', 0, 0, tiled=True)  21.2 us
    all_to_all x1, starting transfers between devices, body(): lax.all_to_all(partial, 'filt', 0, 0, tiled=True)  10 us
    all_to_all x1, waiting for transfers between devices, body(): full = lax.all_to_all(everyone, 'space', 0, 0, tiled=True)  9.8 us
    all_to_all x1, starting transfers between devices, body(): full = lax.all_to_all(everyone, 'space', 0, 0, tiled=True)  6.18 us
    ppermute x1, waiting for transfers between devices, halo_rows(): before = lax.ppermute(array[:, -COLS:], 'space', up)  5.74 us
    ppermute x1, starting transfers between devices, halo_rows(): after = lax.ppermute(array[:, :COLS], 'space', down)  3.91 us
  transfers between devices with their start and end apart: 4, of which 3 were waited for; matrix products, arithmetic and copies ran while one was open for 4% of the time, Pallas kernels for 0%

profile of v1, /device:TPU:64, one launch (start us, length us, event | category | flops | bytes accessed | tf_op | source)
XLA Modules:
  0.0 97.6 jit_solution(15599331631518945602)
XLA Ops:
  0.6 0.0 copy-start
  0.6 1.0 fusion.12
  1.6 3.9 %collective-permute-start.1 = (bf16[32,1024]{1,0:T(8,128)(2,1)S(1)}, bf16[32,1024]{1,0:T(8,128)(2,1)S(1)}, u32[]{:S(2)}, u32[]{:S(2)}) collective-permute-start(bf16[32,1024]{1,0:T(8,128)(2,1)S(1)} %get-tuple-element.4), channel_id=1, source_target_pairs={{8,0},{16,8},{24,16},{32,24},{40,32},{48,40},{56,48},{64,56},{72,6... | collective-permute-start | bytes 196616 | tf_op jit(solution)/shard_map/ppermute | solution.py:16
  5.5 1.9 %collective-permute-start = (bf16[32,1024]{1,0:T(8,128)(2,1)S(1)}, bf16[32,1024]{1,0:T(8,128)(2,1)S(1)}, u32[]{:S(2)}, u32[]{:S(2)}) collective-permute-start(bf16[32,1024]{1,0:T(8,128)(2,1)S(1)} %get-tuple-element.5), channel_id=1, source_target_pairs={{0,8},{8,16},{16,24},{24,32},{32,40},{40,48},{48,56},{56,64},{64,7... | collective-permute-start | bytes 196616 | tf_op jit(solution)/shard_map/ppermute | solution.py:15
  7.5 5.7 %collective-permute-done = bf16[32,1024]{1,0:T(8,128)(2,1)S(1)} collective-permute-done((bf16[32,1024]{1,0:T(8,128)(2,1)S(1)}, bf16[32,1024]{1,0:T(8,128)(2,1)S(1)}, u32[]{:S(2)}, u32[]{:S(2)}) %collective-permute-start) | collective-permute-done | bytes 65568 | tf_op jit(solution)/shard_map/ppermute | solution.py:15
  13.2 0.9 constant_dynamic-update-slice_fusion.1
  14.1 0.0 collective-permute-done.1
  14.2 0.0 copy-start.1
  14.2 0.1 fusion.11
  14.3 0.1 slice.91
  14.4 0.2 maximum_select_fusion
  14.6 0.5 copy-done.1
  15.2 0.5 fusion.1
  15.7 0.0 copy-start.2
  15.8 21.2 %all_to_all.19 = bf16[64,16,128]{2,1,0:T(8,128)(2,1)S(1)} all-to-all(bf16[64,16,128]{2,1,0:T(8,128)(2,1)S(1)} %fusion.3), channel_id=1, replica_groups=mesh['space'=64,'filt'=8] {'space'}, dimensions={0} | all-to-all | bytes 524288 | tf_op jit(solution)/shard_map/all_to_all | solution.py:50
  37.0 0.1 reduce_sum.25
  37.1 0.7 broadcast_in_dim.27
  37.8 6.2 %all-to-all-start.2 = ((bf16[64,16,128]{2,1,0:T(8,128)(2,1)}), bf16[64,16,128]{2,1,0:T(8,128)(2,1)S(1)}, u32[]{:S(2)}, u32[]{:S(2)}) async-start(bf16[64,16,128]{2,1,0:T(8,128)(2,1)} %broadcast_in_dim.27), calls=%async_computation.2 | async-start | bytes 524288 | tf_op jit(solution)/shard_map/all_to_all | solution.py:53
  44.0 1.7 %convolution_convert_fusion = bf16[2048,256]{0,1:T(8,128)(2,1)} fusion(bf16[288,2048]{1,0:T(8,128)(2,1)S(1)} %slice_dynamic-update-slice_fusion, bf16[288,256]{1,0:T(8,128)(2,1)S(1)} %bitcast.26), kind=kOutput, calls=%fused_computation | convolution fusion | flops 302514176 | bytes 2375680 | tf_op jit(solution)/shard_map/dot_general | solution.py:59
  45.8 9.8 %all-to-all-done.2 = bf16[64,16,128]{2,1,0:T(8,128)(2,1)S(1)} async-done(((bf16[64,16,128]{2,1,0:T(8,128)(2,1)}), bf16[64,16,128]{2,1,0:T(8,128)(2,1)S(1)}, u32[]{:S(2)}, u32[]{:S(2)}) %all-to-all-start.2) | async-done | bytes 262176 | tf_op jit(solution)/shard_map/all_to_all | solution.py:53
  55.6 10.0 %all-to-all-start = ((bf16[8,32,2048]{2,1,0:T(8,128)(2,1)}), bf16[8,32,2048]{2,1,0:T(8,128)(2,1)S(1)}, u32[]{:S(2)}, u32[]{:S(2)}) async-start(bf16[8,32,2048]{2,1,0:T(8,128)(2,1)} %bitcast.3), calls=%async_computation | async-start | bytes 2097152 | tf_op jit(solution)/shard_map/all_to_all | solution.py:61
  65.7 0.7 convert.6
  66.4 30.4 %all-to-all-done = bf16[8,32,2048]{2,1,0:T(8,128)(2,1)S(1)} async-done(((bf16[8,32,2048]{2,1,0:T(8,128)(2,1)}), bf16[8,32,2048]{2,1,0:T(8,128)(2,1)S(1)}, u32[]{:S(2)}, u32[]{:S(2)}) %all-to-all-start) | async-done | bytes 1048608 | tf_op jit(solution)/shard_map/all_to_all | solution.py:61
  96.8 0.8 reduce_sum.24
  (22 shorter events, 0.2 us)
Async XLA Ops:
  0.6 14.6 %copy-start = (bf16[256,2048]{1,0:T(8,128)(2,1)S(1)}, bf16[256,2048]{1,0:T(8,128)(2,1)}, u32[]{:S(2)}) copy-start(bf16[256,2048]{1,0:T(8,128)(2,1)} %param.3) | copy-start | bytes 3145732
  1.6 12.5 %collective-permute-start.1 = (bf16[32,1024]{1,0:T(8,128)(2,1)S(1)}, bf16[32,1024]{1,0:T(8,128)(2,1)S(1)}, u32[]{:S(2)}, u32[]{:S(2)}) collective-permute-start(bf16[32,1024]{1,0:T(8,128)(2,1)S(1)} %get-tuple-element.4), channel_id=1, source_target_pairs={{8,0},{16,8},{24,16},{32,24},{40,32},{48,40},{56,48},{64,56},{72,6... | collective-permute-start | bytes 196616 | tf_op jit(solution)/shard_map/ppermute | solution.py:16
  5.5 7.7 %collective-permute-start = (bf16[32,1024]{1,0:T(8,128)(2,1)S(1)}, bf16[32,1024]{1,0:T(8,128)(2,1)S(1)}, u32[]{:S(2)}, u32[]{:S(2)}) collective-permute-start(bf16[32,1024]{1,0:T(8,128)(2,1)S(1)} %get-tuple-element.5), channel_id=1, source_target_pairs={{0,8},{8,16},{16,24},{24,32},{32,40},{40,48},{48,56},{56,64},{64,7... | collective-permute-start | bytes 196616 | tf_op jit(solution)/shard_map/ppermute | solution.py:15
  14.2 0.9 copy-start.1
  15.7 28.3 %copy-start.2 = (bf16[32,3,3,256]{3,0,2,1:T(8,128)(2,1)S(1)}, bf16[32,3,3,256]{3,0,2,1:T(8,128)(2,1)}, u32[]{:S(2)}) copy-start(bf16[32,3,3,256]{3,0,2,1:T(8,128)(2,1)} %param.5) | copy-start | bytes 442372
  37.8 17.7 %all-to-all-start.2 = ((bf16[64,16,128]{2,1,0:T(8,128)(2,1)}), bf16[64,16,128]{2,1,0:T(8,128)(2,1)S(1)}, u32[]{:S(2)}, u32[]{:S(2)}) async-start(bf16[64,16,128]{2,1,0:T(8,128)(2,1)} %broadcast_in_dim.27), calls=%async_computation.2 | async-start | bytes 524288 | tf_op jit(solution)/shard_map/all_to_all | solution.py:53
  55.6 41.2 %all-to-all-start = ((bf16[8,32,2048]{2,1,0:T(8,128)(2,1)}), bf16[8,32,2048]{2,1,0:T(8,128)(2,1)S(1)}, u32[]{:S(2)}, u32[]{:S(2)}) async-start(bf16[8,32,2048]{2,1,0:T(8,128)(2,1)} %bitcast.3), calls=%async_computation | async-start | bytes 2097152 | tf_op jit(solution)/shard_map/all_to_all | solution.py:61

commit v2 on v1

--- a/solution.py
+++ b/solution.py
@@ -38,8 +38,16 @@
     filters = out_grad.shape[0]
     n_space = lax.axis_size("space")
     n_filt = lax.axis_size("filt")
+    n_x = n_filt // 2
     scale = 1.0 / math.sqrt(pixels * n_space)
     before, after = halo_rows(out_grad)
+
+    me = lax.axis_index("filt")
+    here, half = me // 2, me % 2
+    taps = kernel.transpose(3, 1, 2, 0).reshape(n_x, 2, channels // n_filt, 9 * filters)
+    taps = lax.dynamic_slice_in_dim(jnp.concatenate([taps, taps], axis=0), here, n_x, axis=0)
+    taps = jnp.where(half == 1, taps[:, ::-1], taps).reshape(n_x, 2 * (channels // n_filt), 9 * filters)
+
     stack = shifted_stack(out_grad, before, after)
     terms = lax.dot_general(stack, activations, (((1,), (1,)), ((), ())), preferred_element_type=jnp.float32)
     terms = (terms * scale).astype(jnp.bfloat16)
@@ -48,18 +56,32 @@
     high = jnp.pad(tiles[64:], ((0, 56), (0, 0), (0, 0)))
     chunks = jnp.concatenate([low, high], axis=1)
     got = lax.all_to_all(chunks, "space", 0, 0, tiled=True)
+
+    own = None
+    arrived = []
+    for k in range(n_x):
+        part = lax.dot_general(taps[k], stack, (((1,), (0,)), ((), ())), preferred_element_type=jnp.float32)
+        part = part.astype(jnp.bfloat16)
+        if k == 0:
+            own = part
+        else:
+            pairs = [(i, (i + 2 * k) % n_filt) for i in range(n_filt)]
+            arrived.append(lax.ppermute(part, "filt", pairs))
+
     total = jnp.sum(got.astype(jnp.float32), axis=0).astype(jnp.bfloat16)
     everyone = jnp.broadcast_to(total[None], (n_space,) + total.shape)
     full = lax.all_to_all(everyone, "space", 0, 0, tiled=True)
+
+    summed = own.astype(jnp.float32)
+    for other in arrived:
+        summed = summed + other.astype(jnp.float32)
+    keep, give = jnp.split(summed, 2, axis=0)
+    swapped = lax.ppermute(give.astype(jnp.bfloat16), "filt", [(i, i ^ 1) for i in range(n_filt)])
+    input_grad = (keep + swapped.astype(jnp.float32)).astype(jnp.bfloat16)
+
     full = jnp.concatenate([full[:, :8], full[:8, 8:]], axis=0).astype(jnp.float32)
     weight = full.reshape(36, 2, 8, 128).transpose(0, 2, 1, 3).reshape(3, 3, filters, channels)
     weight_grad = weight.transpose(2, 0, 1, 3)
-
-    taps = kernel.transpose(1, 2, 0, 3).reshape(9 * filters, channels)
-    partial = lax.dot_general(taps, stack, (((0,), (0,)), ((), ())), preferred_element_type=jnp.float32)
-    partial = partial.astype(jnp.bfloat16)
-    shares = lax.all_to_all(partial, "filt", 0, 0, tiled=True).reshape(n_filt, channels // n_filt, pixels)
-    input_grad = jnp.sum(shares.astype(jnp.float32), axis=0).astype(jnp.bfloat16)
     return (input_grad, weight_grad)
 
 

time: 98 us -> 77.1 us (0.79)
  the two profiles are of different devices: /device:TPU:64 before, /device:TPU:1 now
where the time goes in v2:
time: 77.1 us; the launch traced here: 76.7 us
  starting transfers between devices  49.5 us (64%)
  waiting for transfers between devices  13.8 us (18%)
  local copies, waits for them, and re-layouts  5.3 us (7%)
  matrix products  4.46 us (6%)
  other arithmetic  2.59 us (3%)
  between operations  1.06 us (1%)
    all_to_all x1, starting transfers between devices, body(): got = lax.all_to_all(chunks, 'space', 0, 0, tiled=True)  14.2 us
    all_to_all x1, waiting for transfers between devices, body(): full = lax.all_to_all(everyone, 'space', 0, 0, tiled=True)  11.6 us
    all_to_all x1, starting transfers between devices, body(): full = lax.all_to_all(everyone, 'space', 0, 0, tiled=True)  8.84 us
    ppermute x3, starting transfers between devices, body(): arrived.append(lax.ppermute(part, 'filt', pairs))  8.39 us
    ppermute x1, starting transfers between devices, body(): lax.ppermute(give.astype(jnp.bfloat16), 'filt', [(i, i ^ 1) for i in rang...  7.94 us
    ppermute x1, starting transfers between devices, halo_rows(): after = lax.ppermute(array[:, :COLS], 'space', down)  5.49 us
    ppermute x1, starting transfers between devices, halo_rows(): before = lax.ppermute(array[:, -COLS:], 'space', up)  4.59 us
    dot_general x4, matrix products, body(): lax.dot_general(taps[k], stack, (((1,), (0,)), ((), ())), preferred_eleme...  3.95 us
  transfers between devices with their start and end apart: 8, of which 2 were waited for; matrix products, arithmetic and copies ran while one was open for 11% of the time, Pallas kernels for 0%

profile of v2, /device:TPU:1, one launch (start us, length us, event | category | flops | bytes accessed | tf_op | source)
XLA Modules:
  0.0 76.7 jit_solution(1903409842132129652)
XLA Ops:
  0.6 1.0 %fusion.19 = (bf16[32,1024]{1,0:T(8,128)(2,1)S(1)}, bf16[32,1024]{1,0:T(8,128)(2,1)S(1)}) fusion(bf16[32,2048]{1,0:T(8,128)(2,1)} %param.4), kind=kLoop, calls=%fused_computation.47 | loop fusion | bytes 262144 | tf_op jit(solution)/shard_map/slice | solution.py:16
  1.6 4.6 %collective-permute-start = (bf16[32,1024]{1,0:T(8,128)(2,1)S(1)}, bf16[32,1024]{1,0:T(8,128)(2,1)S(1)}, u32[]{:S(2)}, u32[]{:S(2)}) collective-permute-start(bf16[32,1024]{1,0:T(8,128)(2,1)S(1)} %get-tuple-element.9), channel_id=1, source_target_pairs={{0,8},{8,16},{16,24},{24,32},{32,40},{40,48},{48,56},{56,64},{64,7... | collective-permute-start | bytes 196616 | tf_op jit(solution)/shard_map/ppermute | solution.py:15
  6.2 5.5 %collective-permute-start.1 = (bf16[32,1024]{1,0:T(8,128)(2,1)S(1)}, bf16[32,1024]{1,0:T(8,128)(2,1)S(1)}, u32[]{:S(2)}, u32[]{:S(2)}) collective-permute-start(bf16[32,1024]{1,0:T(8,128)(2,1)S(1)} %get-tuple-element.8), channel_id=1, source_target_pairs={{8,0},{16,8},{24,16},{32,24},{40,32},{48,40},{56,48},{64,56},{72,6... | collective-permute-start | bytes 196616 | tf_op jit(solution)/shard_map/ppermute | solution.py:16
  11.7 1.3 %reshape.51 = bf16[4,2,32,288]{2,1,0,3:T(2,128)(2,1)S(1)} reshape(bf16[256,3,3,32]{0,3,2,1:T(8,128)(2,1)} %bitcast.40) | data formatting | bytes 294912 | tf_op jit(solution)/shard_map/reshape | solution.py:47
  13.0 0.6 copy.9
  13.8 0.6 fusion.18
  15.1 0.5 fusion.5
  15.7 0.4 convolution_convert_fusion.2
  16.1 1.9 %collective-permute-start.2 = (bf16[64,2048]{1,0:T(8,128)(2,1)S(1)}, bf16[64,2048]{1,0:T(8,128)(2,1)S(1)}, u32[]{:S(2)}, u32[]{:S(2)}) collective-permute-start(bf16[64,2048]{1,0:T(8,128)(2,1)S(1)} %convolution_convert_fusion.2), channel_id=1, source_target_pairs={{0,2},{1,3},{2,4},{3,5},{4,6},{5,7},{6,0},{7,1},{8,10},{9,11},{10,... | collective-permute-start | bytes 786440 | tf_op jit(solution)/shard_map/ppermute | solution.py:69
  18.0 1.1 %convolution_convert_fusion.1 = bf16[64,2048]{1,0:T(8,128)(2,1)} fusion(bf16[64,288]{1,0:T(8,128)(2,1)S(1)} %bitcast.37, bf16[288,2048]{1,0:T(8,128)(2,1)S(1)} %slice_dynamic-update-slice_fusion), kind=kOutput, calls=%fused_computation.1 | convolution fusion | flops 75628544 | bytes 1478656 | tf_op jit(solution)/shard_map/dot_general | solution.py:63
  19.1 2.8 %collective-permute-start.3 = (bf16[64,2048]{1,0:T(8,128)(2,1)}, bf16[64,2048]{1,0:T(8,128)(2,1)S(1)}, u32[]{:S(2)}, u32[]{:S(2)}) collective-permute-start(bf16[64,2048]{1,0:T(8,128)(2,1)} %convolution_convert_fusion.1), channel_id=1, source_target_pairs={{0,4},{1,5},{2,6},{3,7},{4,0},{5,1},{6,2},{7,3},{8,12},{9,13},{10,... | collective-permute-start | bytes 786440 | tf_op jit(solution)/shard_map/ppermute | solution.py:69
  21.9 1.1 %convolution_convert_fusion = bf16[64,2048]{1,0:T(8,128)(2,1)} fusion(bf16[64,288]{1,0:T(8,128)(2,1)S(1)} %bitcast.36, bf16[288,2048]{1,0:T(8,128)(2,1)S(1)} %slice_dynamic-update-slice_fusion), kind=kOutput, calls=%fused_computation | convolution fusion | flops 75628544 | bytes 1478656 | tf_op jit(solution)/shard_map/dot_general | solution.py:63
  23.0 3.7 %collective-permute-start.4 = (bf16[64,2048]{1,0:T(8,128)(2,1)}, bf16[64,2048]{1,0:T(8,128)(2,1)S(1)}, u32[]{:S(2)}, u32[]{:S(2)}) collective-permute-start(bf16[64,2048]{1,0:T(8,128)(2,1)} %convolution_convert_fusion), channel_id=1, source_target_pairs={{0,6},{1,7},{2,0},{3,1},{4,2},{5,3},{6,4},{7,5},{8,14},{9,15},{10,... | collective-permute-start | bytes 786440 | tf_op jit(solution)/shard_map/ppermute | solution.py:69
  26.7 0.7 fusion.7
  27.4 14.2 %all-to-all-start = ((bf16[64,16,128]{2,1,0:T(8,128)(2,1)}), bf16[64,16,128]{2,1,0:T(8,128)(2,1)S(1)}, u32[]{:S(2)}, u32[]{:S(2)}) async-start(bf16[64,16,128]{2,1,0:T(8,128)(2,1)} %fusion.7), calls=%async_computation | async-start | bytes 524288 | tf_op jit(solution)/shard_map/all_to_all | solution.py:58
  41.7 0.7 copy-done.3
  42.4 1.4 %fusion.3 = f32[64,2048]{1,0:T(8,128)S(1)} fusion(bf16[64,288]{1,0:T(8,128)(2,1)} %bitcast.39, bf16[288,2048]{1,0:T(8,128)(2,1)S(1)} %slice_dynamic-update-slice_fusion, bf16[64,2048]{1,0:T(8,128)(2,1)} %copy-done.3, bf16[64,2048]{1,0:T(8,128)(2,1)S(1)} %collective-permute-done.3, bf16[64,2048]{1,0:T(8,128)(2,1)S(1)} %collective-permute-done.2), kind=kOutput, calls=%fused_computation.7 | convolution fusion | flops 76546048 | bytes 2527232 | tf_op jit(solution)/shard_map/dot_general | solution.py:63
  43.8 7.9 %collective-permute-start.5 = (bf16[32,2048]{1,0:T(8,128)(2,1)S(1)}, bf16[32,2048]{1,0:T(8,128)(2,1)S(1)}, u32[]{:S(2)}, u32[]{:S(2)}) collective-permute-start(bf16[32,2048]{1,0:T(8,128)(2,1)S(1)} %split.15), channel_id=1, source_target_pairs={{0,1},{1,0},{2,3},{3,2},{4,5},{5,4},{6,7},{7,6},{8,9},{9,8},{10,11... | collective-permute-start | bytes 393224 | tf_op jit(solution)/shard_map/ppermute | solution.py:79
  51.8 2.2 %all-to-all-done = bf16[64,16,128]{2,1,0:T(8,128)(2,1)S(1)} async-done(((bf16[64,16,128]{2,1,0:T(8,128)(2,1)}), bf16[64,16,128]{2,1,0:T(8,128)(2,1)S(1)}, u32[]{:S(2)}, u32[]{:S(2)}) %all-to-all-start) | async-done | bytes 262176 | tf_op jit(solution)/shard_map/all_to_all | solution.py:58
  54.0 0.7 broadcast_in_dim.27
  54.8 8.8 %all-to-all-start.1 = ((bf16[64,16,128]{2,1,0:T(8,128)(2,1)}), bf16[64,16,128]{2,1,0:T(8,128)(2,1)S(1)}, u32[]{:S(2)}, u32[]{:S(2)}) async-start(bf16[64,16,128]{2,1,0:T(8,128)(2,1)} %broadcast_in_dim.27), calls=%async_computation.1 | async-start | bytes 524288 | tf_op jit(solution)/shard_map/all_to_all | solution.py:73
  63.6 0.7 fusion.8
  64.3 11.6 %all-to-all-done.1 = bf16[64,16,128]{2,1,0:T(8,128)(2,1)S(1)} async-done(((bf16[64,16,128]{2,1,0:T(8,128)(2,1)}), bf16[64,16,128]{2,1,0:T(8,128)(2,1)S(1)}, u32[]{:S(2)}, u32[]{:S(2)}) %all-to-all-start.1) | async-done | bytes 262176 | tf_op jit(solution)/shard_map/all_to_all | solution.py:73
  75.9 0.7 convert.9
  (42 shorter events, 0.8 us)
Async XLA Ops:
  0.6 14.5 %copy-start = (bf16[256,2048]{1,0:T(8,128)(2,1)S(1)}, bf16[256,2048]{1,0:T(8,128)(2,1)}, u32[]{:S(2)}) copy-start(bf16[256,2048]{1,0:T(8,128)(2,1)} %param.3) | copy-start | bytes 3145732
  1.6 12.9 %collective-permute-start = (bf16[32,1024]{1,0:T(8,128)(2,1)S(1)}, bf16[32,1024]{1,0:T(8,128)(2,1)S(1)}, u32[]{:S(2)}, u32[]{:S(2)}) collective-permute-start(bf16[32,1024]{1,0:T(8,128)(2,1)S(1)} %get-tuple-element.9), channel_id=1, source_target_pairs={{0,8},{8,16},{16,24},{24,32},{32,40},{40,48},{48,56},{56,64},{64,7... | collective-permute-start | bytes 196616 | tf_op jit(solution)/shard_map/ppermute | solution.py:15
  6.2 8.3 %collective-permute-start.1 = (bf16[32,1024]{1,0:T(8,128)(2,1)S(1)}, bf16[32,1024]{1,0:T(8,128)(2,1)S(1)}, u32[]{:S(2)}, u32[]{:S(2)}) collective-permute-start(bf16[32,1024]{1,0:T(8,128)(2,1)S(1)} %get-tuple-element.8), channel_id=1, source_target_pairs={{8,0},{16,8},{24,16},{32,24},{40,32},{48,40},{56,48},{64,56},{72,6... | collective-permute-start | bytes 196616 | tf_op jit(solution)/shard_map/ppermute | solution.py:16
  13.0 1.5 %copy-start.1 = (bf16[32,2048]{1,0:T(8,128)(2,1)S(1)}, bf16[32,2048]{1,0:T(8,128)(2,1)}, u32[]{:S(2)}) copy-start(bf16[32,2048]{1,0:T(8,128)(2,1)} %param.4) | copy-start | bytes 393220
  15.7 3.4 %copy-start.2 = (bf16[36,2,8,128]{3,2,1,0:T(8,128)(2,1)}, bf16[36,2,8,128]{3,2,1,0:T(8,128)(2,1)S(1)}, u32[]{:S(2)}) copy-start(bf16[36,2,8,128]{3,2,1,0:T(8,128)(2,1)S(1)} %fusion.5) | copy-start | bytes 442372
  16.1 25.6 %collective-permute-start.2 = (bf16[64,2048]{1,0:T(8,128)(2,1)S(1)}, bf16[64,2048]{1,0:T(8,128)(2,1)S(1)}, u32[]{:S(2)}, u32[]{:S(2)}) collective-permute-start(bf16[64,2048]{1,0:T(8,128)(2,1)S(1)} %convolution_convert_fusion.2), channel_id=1, source_target_pairs={{0,2},{1,3},{2,4},{3,5},{4,6},{5,7},{6,0},{7,1},{8,10},{9,11},{10,... | collective-permute-start | bytes 786440 | tf_op jit(solution)/shard_map/ppermute | solution.py:69
  19.1 22.6 %collective-permute-start.3 = (bf16[64,2048]{1,0:T(8,128)(2,1)}, bf16[64,2048]{1,0:T(8,128)(2,1)S(1)}, u32[]{:S(2)}, u32[]{:S(2)}) collective-permute-start(bf16[64,2048]{1,0:T(8,128)(2,1)} %convolution_convert_fusion.1), channel_id=1, source_target_pairs={{0,4},{1,5},{2,6},{3,7},{4,0},{5,1},{6,2},{7,3},{8,12},{9,13},{10,... | collective-permute-start | bytes 786440 | tf_op jit(solution)/shard_map/ppermute | solution.py:69
  21.9 4.8 %slice-start = ((bf16[36,2,8,128]{3,2,1,0:T(8,128)(2,1)}), bf16[32,2,8,128]{3,2,1,0:T(8,128)(2,1)S(1)}, s32[]{:S(2)}) async-start(bf16[36,2,8,128]{3,2,1,0:T(8,128)(2,1)} %copy-done.2), calls=%async_computation.2 | async-start | bytes 262144 | tf_op jit(solution)/shard_map/slice | solution.py:55
  21.9 4.8 %slice-start.1 = ((bf16[36,2,8,128]{3,2,1,0:T(8,128)(2,1)}), bf16[4,2,8,128]{3,2,1,0:T(8,128)(2,1)S(1)}, s32[]{:S(2)}) async-start(bf16[36,2,8,128]{3,2,1,0:T(8,128)(2,1)} %copy-done.2), calls=%async_computation.3 | async-start | bytes 32768 | tf_op jit(solution)/shard_map/slice | solution.py:56
  23.0 18.7 %collective-permute-start.4 = (bf16[64,2048]{1,0:T(8,128)(2,1)}, bf16[64,2048]{1,0:T(8,128)(2,1)S(1)}, u32[]{:S(2)}, u32[]{:S(2)}) collective-permute-start(bf16[64,2048]{1,0:T(8,128)(2,1)} %convolution_convert_fusion), channel_id=1, source_target_pairs={{0,6},{1,7},{2,0},{3,1},{4,2},{5,3},{6,4},{7,5},{8,14},{9,15},{10,... | collective-permute-start | bytes 786440 | tf_op jit(solution)/shard_map/ppermute | solution.py:69
  27.4 26.5 %all-to-all-start = ((bf16[64,16,128]{2,1,0:T(8,128)(2,1)}), bf16[64,16,128]{2,1,0:T(8,128)(2,1)S(1)}, u32[]{:S(2)}, u32[]{:S(2)}) async-start(bf16[64,16,128]{2,1,0:T(8,128)(2,1)} %fusion.7), calls=%async_computation | async-start | bytes 524288 | tf_op jit(solution)/shard_map/all_to_all | solution.py:58
  41.7 0.7 copy-start.3
  43.8 19.8 %collective-permute-start.5 = (bf16[32,2048]{1,0:T(8,128)(2,1)S(1)}, bf16[32,2048]{1,0:T(8,128)(2,1)S(1)}, u32[]{:S(2)}, u32[]{:S(2)}) collective-permute-start(bf16[32,2048]{1,0:T(8,128)(2,1)S(1)} %split.15), channel_id=1, source_target_pairs={{0,1},{1,0},{2,3},{3,2},{4,5},{5,4},{6,7},{7,6},{8,9},{9,8},{10,11... | collective-permute-start | bytes 393224 | tf_op jit(solution)/shard_map/ppermute | solution.py:79
  54.8 21.1 %all-to-all-start.1 = ((bf16[64,16,128]{2,1,0:T(8,128)(2,1)}), bf16[64,16,128]{2,1,0:T(8,128)(2,1)S(1)}, u32[]{:S(2)}, u32[]{:S(2)}) async-start(bf16[64,16,128]{2,1,0:T(8,128)(2,1)} %broadcast_in_dim.27), calls=%async_computation.1 | async-start | bytes 524288 | tf_op jit(solution)/shard_map/all_to_all | solution.py:73

commit v3 on v2

v3 whole, which is shorter than its diff:
```python
import functools
import math

import jax
import jax.numpy as jnp
from jax import lax
from jax.experimental import pallas as pl
from jax.experimental.pallas import tpu as pltpu
from jax.sharding import PartitionSpec as P

COLS = 1024
VMEM = pl.BlockSpec(memory_space=pltpu.VMEM)
SMEM = pl.BlockSpec(memory_space=pltpu.SMEM)


def cost(flops):
    return pl.CostEstimate(flops=flops, bytes_accessed=1 << 20, transcendentals=0)


def halo_rows(array):
    size = lax.axis_size("space")
    up = [(i, i + 1) for i in range(size - 1)]
    down = [(j, i) for i, j in up]
    before = lax.ppermute(array[:, -COLS:], "space", up)
    after = lax.ppermute(array[:, :COLS], "space", down)
    return before, after


def shifted_stack(out_grad, before, after):
    filters, pixels = out_grad.shape
    rows = jnp.concatenate([before, out_grad, after], axis=1)
    column = lax.broadcasted_iota(jnp.int32, (1, rows.shape[1]), 1) % COLS
    zero = jnp.zeros((), rows.dtype)
    right = jnp.where(column == 0, zero, jnp.roll(rows, 1, axis=1))
    left = jnp.where(column == COLS - 1, zero, jnp.roll(rows, -1, axis=1))
    by_col = {-1: right, 0: rows, 1: left}
    stack = []
    for i in range(3):
        for j in range(3):
            start = COLS * (2 - i)
            stack.append(by_col[1 - j][:, start:start + pixels])
    return jnp.concatenate(stack, axis=0)


def parts_kernel(n_x, share, where_ref, taps_ref, stack_ref, *rest):
    outs, turned, order = rest[:n_x], rest[n_x], rest[n_x + 1]
    turned[...] = taps_ref[...].astype(jnp.float32).T.astype(jnp.bfloat16)
    here, half = where_ref[0], where_ref[1]
    for k in range(n_x):
        block = lax.rem(here + k, n_x) * 2
        for h in range(2):
            start = pl.multiple_of((block + lax.rem(half + h, 2)) * share, share)
            order[(2 * k + h) * share:(2 * k + h + 1) * share, :] = turned[pl.ds(start, share), :]
    wide = 512
    for c in range(stack_ref.shape[1] // wide):
        cols = slice(c * wide, c * wide + wide)
        got = jnp.dot(order[...], stack_ref[:, cols], preferred_element_type=jnp.float32).astype(jnp.bfloat16)
        for k in range(n_x):
            outs[k][:, cols] = got[2 * k * share:2 * (k + 1) * share, :]


def sum_kernel(got_ref, out_ref):
    total = jnp.sum(got_ref[...].astype(jnp.float32), axis=0).astype(jnp.bfloat16)
    out_ref[...] = jnp.broadcast_to(total[None], out_ref.shape)


def weight_kernel(full_ref, out_ref):
    for d in range(72):
        row, col = d // 2, d % 2
        for g in range(4):
            pair = full_ref[d, g] if d < 64 else full_ref[(d - 64) * 4 + g, 4]
            top = row * 8 + 2 * g
            out_ref[top:top + 2, col * 128:col * 128 + 128] = pair.astype(jnp.float32)


def body(activations, out_grad, kernel):
    channels, pixels = activations.shape
    filters = out_grad.shape[0]
    n_space = lax.axis_size("space")
    n_filt = lax.axis_size("filt")
    n_x = n_filt // 2
    share = channels // n_filt
    scale = 1.0 / math.sqrt(pixels * n_space)
    before, after = halo_rows(out_grad)
    me = lax.axis_index("filt")
    where = jnp.stack([me // 2, me % 2])

    stack = shifted_stack(out_grad, before, after)
    terms = lax.dot_general(stack, activations, (((1,), (1,)), ((), ())), preferred_element_type=jnp.float32)
    terms = (terms * scale).astype(jnp.bfloat16)
    tiles = terms.reshape(36, 8, 2, 128).transpose(0, 2, 1, 3).reshape(72, 8, 128)
    low = tiles[:64].reshape(64, 4, 2, 128)
    high = jnp.pad(tiles[64:].reshape(32, 1, 2, 128), ((0, 32), (0, 0), (0, 0), (0, 0)))
    chunks = jnp.concatenate([low, high], axis=1)
    got = lax.all_to_all(chunks, "space", 0, 0, tiled=True)

    taps = kernel.transpose(1, 2, 0, 3).reshape(9 * filters, channels)
    part = jax.ShapeDtypeStruct((2 * share, pixels), jnp.bfloat16)
    own, *parts = pl.pallas_call(
        functools.partial(parts_kernel, n_x, share),
        out_shape=[part] * n_x,
        in_specs=[SMEM, VMEM, VMEM],
        out_specs=[VMEM] * n_x,
        scratch_shapes=[pltpu.VMEM((channels, 9 * filters), jnp.bfloat16)] * 2,
        cost_estimate=cost(P_COST),
        compiler_params=pltpu.CompilerParams(vmem_limit_bytes=32 << 20),
        name="parts",
    )(where, taps, stack)
    arrived = []
    for k in range(1, n_x):
        pairs = [(i, (i + 2 * k) % n_filt) for i in range(n_filt)]
        arrived.append(lax.ppermute(parts[k - 1], "filt", pairs))

    everyone = pl.pallas_call(
        sum_kernel,
        out_shape=jax.ShapeDtypeStruct(got.shape, jnp.bfloat16),
        in_specs=[VMEM], out_specs=VMEM, cost_estimate=cost(S_COST), name="chunk_sum",
    )(got)
    own, everyone = lax.optimization_barrier((own, everyone))
    full = lax.all_to_all(everyone, "space", 0, 0, tiled=True)

    summed = own.astype(jnp.float32)
    for other in arrived:
        summed = summed + other.astype(jnp.float32)
    keep, give = jnp.split(summed, 2, axis=0)
    swapped = lax.ppermute(give.astype(jnp.bfloat16), "filt", [(i, i ^ 1) for i in range(n_filt)])
    weight = pl.pallas_call(
        weight_kernel,
        out_shape=jax.ShapeDtypeStruct((9 * filters, channels), jnp.float32),
        in_specs=[VMEM], out_specs=VMEM, cost_estimate=cost(W_COST), name="weight_out",
    )(full)
    swapped, weight = lax.optimization_barrier((swapped, weight))
    input_grad = (keep + swapped.astype(jnp.float32)).astype(jnp.bfloat16)

    weight_grad = weight.reshape(3, 3, filters, channels).transpose(2, 0, 1, 3)
    return (input_grad, weight_grad)


P_COST = 115_000_000_000
S_COST = 115_000_000_000
W_COST = 115_000_000_000


def solution(mesh):
    in_specs = (P(None, "space"), P("filt", "space"), P("filt", None, None, None))
    out_specs = (P("filt", "space"), P("filt", None, None, None))
    return jax.shard_map(body, mesh=mesh, in_specs=in_specs, out_specs=out_specs, check_vma=False)
```

time: 77.1 us -> 68.7 us (0.89)
  waiting for transfers between devices: 13.8 us -> 4.46 us
  Pallas kernels: 0 us -> 4.87 us
  matrix products: 4.46 us -> 0.51 us
  starting transfers between devices: 49.5 us -> 52.9 us
  local copies, waits for them, and re-layouts: 5.3 us -> 2.71 us
    all_to_all x1, waiting for transfers between devices: 11.6 us -> 2.02 us  [body(): full = lax.all_to_all(everyone, 'space', 0, 0, tiled=True)]
    pallas_call x0 -> x3, Pallas kernels: none -> 4.87 us  [the longest x1 1.78 us: body(): pl.pallas_call(sum_kernel, out_shape=jax.ShapeDtypeStruct(got.shape, jnp....]
    dot_general x4 -> x0, matrix products: 3.95 us -> none  [body(): lax.dot_general(taps[k], stack, (((1,), (0,)), ((), ())), preferred_eleme...]
    all_to_all x1, starting transfers between devices: 8.84 us -> 11.7 us  [body(): full = lax.all_to_all(everyone, 'space', 0, 0, tiled=True)]
    ppermute x1, waiting for transfers between devices: 0.01 us -> 2.42 us  [body(): lax.ppermute(give.astype(jnp.bfloat16), 'filt', [(i, i ^ 1) for i in rang...]
    all_to_all x1, waiting for transfers between devices: 2.17 us -> 0.01 us  [body(): got = lax.all_to_all(chunks, 'space', 0, 0, tiled=True)]
    ppermute x3, starting transfers between devices: 8.39 us -> 10.5 us  [body(): arrived.append(lax.ppermute(parts[k - 1], 'filt', pairs))]
    reshape x2 -> x0, local copies, waits for them, and re-layouts: 1.88 us -> none  [body(): kernel.transpose(3, 1, 2, 0)]
  transfers between devices with their start and end apart: 8 -> 8, of which waited for: 2 -> 2; matrix products, arithmetic and copies ran while one was open for 11% -> 2% of each run, Pallas kernels for 0% -> 7%
where the time goes in v3:
time: 68.7 us; the launch traced here: 68.3 us
  starting transfers between devices  52.9 us (77%)
  Pallas kernels  4.87 us (7%)
  waiting for transfers between devices  4.46 us (6%)
  local copies, waits for them, and re-layouts  2.71 us (4%)
  other arithmetic  1.9 us (3%)
  between operations  0.96 us (1%)
    all_to_all x1, starting transfers between devices, body(): got = lax.all_to_all(chunks, 'space', 0, 0, tiled=True)  12.6 us
    all_to_all x1, starting transfers between devices, body(): full = lax.all_to_all(everyone, 'space', 0, 0, tiled=True)  11.7 us
    ppermute x3, starting transfers between devices, body(): arrived.append(lax.ppermute(parts[k - 1], 'filt', pairs))  10.5 us
    ppermute x1, starting transfers between devices, body(): lax.ppermute(give.astype(jnp.bfloat16), 'filt', [(i, i ^ 1) for i in rang...  7.94 us
    ppermute x1, starting transfers between devices, halo_rows(): after = lax.ppermute(array[:, :COLS], 'space', down)  5.49 us
    ppermute x1, starting transfers between devices, halo_rows(): before = lax.ppermute(array[:, -COLS:], 'space', up)  4.59 us
    ppermute x1, waiting for transfers between devices, body(): lax.ppermute(give.astype(jnp.bfloat16), 'filt', [(i, i ^ 1) for i in rang...  2.42 us
    all_to_all x1, waiting for transfers between devices, body(): full = lax.all_to_all(everyone, 'space', 0, 0, tiled=True)  2.02 us
  transfers between devices with their start and end apart: 8, of which 2 were waited for; matrix products, arithmetic and copies ran while one was open for 2% of the time, Pallas kernels for 7%

profile of v3, /device:TPU:1, one launch (start us, length us, event | category | flops | bytes accessed | tf_op | source)
XLA Modules:
  0.0 68.3 jit_solution(1262567755752939294)
XLA Ops:
  0.6 1.0 %fusion.12 = (bf16[32,1024]{1,0:T(8,128)(2,1)S(1)}, bf16[32,1024]{1,0:T(8,128)(2,1)S(1)}) fusion(bf16[32,2048]{1,0:T(8,128)(2,1)} %param.4), kind=kLoop, calls=%fused_computation.34 | loop fusion | bytes 262144 | tf_op jit(solution)/shard_map/slice | solution.py:25
  1.6 4.6 %collective-permute-start = (bf16[32,1024]{1,0:T(8,128)(2,1)S(1)}, bf16[32,1024]{1,0:T(8,128)(2,1)S(1)}, u32[]{:S(2)}, u32[]{:S(2)}) collective-permute-start(bf16[32,1024]{1,0:T(8,128)(2,1)S(1)} %get-tuple-element.21), channel_id=1, source_target_pairs={{0,8},{8,16},{16,24},{24,32},{32,40},{40,48},{48,56},{56,64},{64,7... | collective-permute-start | bytes 196616 | tf_op jit(solution)/shard_map/ppermute | solution.py:24
  6.2 5.5 %collective-permute-start.1 = (bf16[32,1024]{1,0:T(8,128)(2,1)S(1)}, bf16[32,1024]{1,0:T(8,128)(2,1)S(1)}, u32[]{:S(2)}, u32[]{:S(2)}) collective-permute-start(bf16[32,1024]{1,0:T(8,128)(2,1)S(1)} %get-tuple-element.20), channel_id=1, source_target_pairs={{8,0},{16,8},{24,16},{32,24},{40,32},{48,40},{56,48},{64,56},{72,6... | collective-permute-start | bytes 196616 | tf_op jit(solution)/shard_map/ppermute | solution.py:25
  11.8 0.1 pad_add_fusion.where_ref
  11.8 0.9 %constant_dynamic-update-slice_fusion.1 = bf16[32,4096]{1,0:T(8,128)(2,1)S(1)} fusion(bf16[32,4096]{1,0:T(8,128)(2,1)S(1)} %constant_dynamic-update-slice_fusion.2, bf16[32,2048]{1,0:T(8,128)(2,1)} %param.4), kind=kLoop, calls=%fused_computation.22 | loop fusion | bytes 262144
  12.8 0.1 fusion.11
  13.0 0.1 slice.77
  13.0 0.2 maximum_select_fusion
  13.2 0.5 copy-done.2
  13.9 0.5 fusion.1
  14.4 0.8 %fusion.3 = bf16[64,5,2,128]{3,2,1,0:T(2,128)(2,1)} fusion(bf16[32,1,2,128]{3,2,1,0:T(2,128)(2,1)S(1)} %bitcast.18, bf16[64,4,2,128]{3,2,1,0:T(2,128)(2,1)S(1)} %bitcast.17), kind=kLoop, calls=%fused_computation.10 | loop fusion | flops 491520 | bytes 311296 | tf_op jit(solution)/shard_map/concatenate | solution.py:94
  15.2 12.6 %all-to-all-start = ((bf16[64,5,2,128]{3,2,1,0:T(2,128)(2,1)}), bf16[64,5,2,128]{3,2,1,0:T(2,128)(2,1)}, u32[]{:S(2)}, u32[]{:S(2)}) async-start(bf16[64,5,2,128]{3,2,1,0:T(2,128)(2,1)} %fusion.3), calls=%async_computation | async-start | bytes 327680 | tf_op jit(solution)/shard_map/all_to_all | solution.py:95
  27.8 1.3 %parts.1 = (bf16[64,2048]{1,0:T(8,128)(2,1)S(1)}, bf16[64,2048]{1,0:T(8,128)(2,1)S(1)}, bf16[64,2048]{1,0:T(8,128)(2,1)S(1)}, bf16[64,2048]{1,0:T(8,128)(2,1)S(1)}) custom-call(s32[2]{0:T(128)S(1)} %pad_add_fusion.where_ref, bf16[288,256]{1,0:T(8,128)(2,1)S(1)} %bitcast.16, bf16[288,2048]{1,0:T(8,128)(2,1)S(1)} %slice_dynamic-update-slice_fusion.stack_ref), custom_call_target="tpu_custom_call" | custom-call | flops 115000000512 | bytes 1048576 | tf_op jit(solution)/shard_map/parts/pallas_call | solution.py:99
  29.2 3.1 %collective-permute-start.2 = (bf16[64,2048]{1,0:T(8,128)(2,1)S(1)}, bf16[64,2048]{1,0:T(8,128)(2,1)S(1)}, u32[]{:S(2)}, u32[]{:S(2)}) collective-permute-start(bf16[64,2048]{1,0:T(8,128)(2,1)S(1)} %get-tuple-element.12), channel_id=1, source_target_pairs={{0,2},{1,3},{2,4},{3,5},{4,6},{5,7},{6,0},{7,1},{8,10},{9,11},{10,... | collective-permute-start | bytes 786440 | tf_op jit(solution)/shard_map/ppermute | solution.py:112
  32.3 4.4 %collective-permute-start.3 = (bf16[64,2048]{1,0:T(8,128)(2,1)S(1)}, bf16[64,2048]{1,0:T(8,128)(2,1)S(1)}, u32[]{:S(2)}, u32[]{:S(2)}) collective-permute-start(bf16[64,2048]{1,0:T(8,128)(2,1)S(1)} %get-tuple-element.13), channel_id=1, source_target_pairs={{0,4},{1,5},{2,6},{3,7},{4,0},{5,1},{6,2},{7,3},{8,12},{9,13},{10,... | collective-permute-start | bytes 786440 | tf_op jit(solution)/shard_map/ppermute | solution.py:112
  36.7 3.1 %collective-permute-start.4 = (bf16[64,2048]{1,0:T(8,128)(2,1)S(1)}, bf16[64,2048]{1,0:T(8,128)(2,1)S(1)}, u32[]{:S(2)}, u32[]{:S(2)}) collective-permute-start(bf16[64,2048]{1,0:T(8,128)(2,1)S(1)} %get-tuple-element.14), channel_id=1, source_target_pairs={{0,6},{1,7},{2,0},{3,1},{4,2},{5,3},{6,4},{7,5},{8,14},{9,15},{10,... | collective-permute-start | bytes 786440 | tf_op jit(solution)/shard_map/ppermute | solution.py:112
  39.7 1.8 %chunk_sum.1 = bf16[64,5,2,128]{3,2,1,0:T(2,128)(2,1)} custom-call(bf16[64,5,2,128]{3,2,1,0:T(2,128)(2,1)} %all-to-all-done.got_ref), custom_call_target="tpu_custom_call" | custom-call | flops 115000000512 | bytes 1048576 | tf_op jit(solution)/shard_map/chunk_sum/pallas_call | solution.py:114
  41.5 11.7 %all-to-all-start.1 = ((bf16[64,5,2,128]{3,2,1,0:T(2,128)(2,1)}), bf16[64,5,2,128]{3,2,1,0:T(2,128)(2,1)}, u32[]{:S(2)}, u32[]{:S(2)}) async-start(bf16[64,5,2,128]{3,2,1,0:T(2,128)(2,1)} %chunk_sum.1), calls=%async_computation.1 | async-start | bytes 327680 | tf_op jit(solution)/shard_map/all_to_all | solution.py:120
  53.3 0.1 convert_add_fusion
  53.5 7.9 %collective-permute-start.5 = (bf16[32,2048]{1,0:T(8,128)(2,1)S(1)}, bf16[32,2048]{1,0:T(8,128)(2,1)S(1)}, u32[]{:S(2)}, u32[]{:S(2)}) collective-permute-start(bf16[32,2048]{1,0:T(8,128)(2,1)S(1)} %split.15), channel_id=1, source_target_pairs={{0,1},{1,0},{2,3},{3,2},{4,5},{5,4},{6,7},{7,6},{8,9},{9,8},{10,11... | collective-permute-start | bytes 393224 | tf_op jit(solution)/shard_map/ppermute | solution.py:126
  61.4 2.0 %all-to-all-done.1.full_ref = bf16[64,5,2,128]{3,2,1,0:T(2,128)(2,1)} async-done(((bf16[64,5,2,128]{3,2,1,0:T(2,128)(2,1)}), bf16[64,5,2,128]{3,2,1,0:T(2,128)(2,1)}, u32[]{:S(2)}, u32[]{:S(2)}) %all-to-all-start.1) | async-done | bytes 163872 | tf_op jit(solution)/shard_map/all_to_all | solution.py:120
  63.4 1.7 %weight_out.1 = f32[288,256]{1,0:T(8,128)} custom-call(bf16[64,5,2,128]{3,2,1,0:T(2,128)(2,1)} %all-to-all-done.1.full_ref), custom_call_target="tpu_custom_call" | custom-call | flops 115000000512 | bytes 1048576 | tf_op jit(solution)/shard_map/weight_out/pallas_call | solution.py:127
  65.2 2.4 %collective-permute-done.5 = bf16[32,2048]{1,0:T(8,128)(2,1)S(1)} collective-permute-done((bf16[32,2048]{1,0:T(8,128)(2,1)S(1)}, bf16[32,2048]{1,0:T(8,128)(2,1)S(1)}, u32[]{:S(2)}, u32[]{:S(2)}) %collective-permute-start.5) | collective-permute-done | bytes 131104 | tf_op jit(solution)/shard_map/ppermute | solution.py:126
  67.6 0.7 fusion.2
  (28 shorter events, 0.2 us)
Async XLA Ops:
  0.6 13.2 %copy-start = (bf16[256,2048]{1,0:T(8,128)(2,1)S(1)}, bf16[256,2048]{1,0:T(8,128)(2,1)}, u32[]{:S(2)}) copy-start(bf16[256,2048]{1,0:T(8,128)(2,1)} %param.3) | copy-start | bytes 3145732
  1.6 10.2 %collective-permute-start = (bf16[32,1024]{1,0:T(8,128)(2,1)S(1)}, bf16[32,1024]{1,0:T(8,128)(2,1)S(1)}, u32[]{:S(2)}, u32[]{:S(2)}) collective-permute-start(bf16[32,1024]{1,0:T(8,128)(2,1)S(1)} %get-tuple-element.21), channel_id=1, source_target_pairs={{0,8},{8,16},{16,24},{24,32},{32,40},{40,48},{48,56},{56,64},{64,7... | collective-permute-start | bytes 196616 | tf_op jit(solution)/shard_map/ppermute | solution.py:24
  6.2 6.5 %collective-permute-start.1 = (bf16[32,1024]{1,0:T(8,128)(2,1)S(1)}, bf16[32,1024]{1,0:T(8,128)(2,1)S(1)}, u32[]{:S(2)}, u32[]{:S(2)}) collective-permute-start(bf16[32,1024]{1,0:T(8,128)(2,1)S(1)} %get-tuple-element.20), channel_id=1, source_target_pairs={{8,0},{16,8},{24,16},{32,24},{40,32},{48,40},{56,48},{64,56},{72,6... | collective-permute-start | bytes 196616 | tf_op jit(solution)/shard_map/ppermute | solution.py:25
  12.8 0.9 %copy-start.2 = (bf16[32,2048]{1,0:T(8,128)(2,1)S(1)}, bf16[32,2048]{1,0:T(8,128)(2,1)}, u32[]{:S(2)}) copy-start(bf16[32,2048]{1,0:T(8,128)(2,1)} %param.4) | copy-start | bytes 393220
  13.9 14.0 %copy-start.1 = (bf16[32,3,3,256]{3,0,2,1:T(8,128)(2,1)S(1)}, bf16[32,3,3,256]{3,0,2,1:T(8,128)(2,1)}, u32[]{:S(2)}) copy-start(bf16[32,3,3,256]{3,0,2,1:T(8,128)(2,1)} %param.5) | copy-start | bytes 442372
  15.2 24.5 %all-to-all-start = ((bf16[64,5,2,128]{3,2,1,0:T(2,128)(2,1)}), bf16[64,5,2,128]{3,2,1,0:T(2,128)(2,1)}, u32[]{:S(2)}, u32[]{:S(2)}) async-start(bf16[64,5,2,128]{3,2,1,0:T(2,128)(2,1)} %fusion.3), calls=%async_computation | async-start | bytes 327680 | tf_op jit(solution)/shard_map/all_to_all | solution.py:95
  29.2 24.1 %collective-permute-start.2 = (bf16[64,2048]{1,0:T(8,128)(2,1)S(1)}, bf16[64,2048]{1,0:T(8,128)(2,1)S(1)}, u32[]{:S(2)}, u32[]{:S(2)}) collective-permute-start(bf16[64,2048]{1,0:T(8,128)(2,1)S(1)} %get-tuple-element.12), channel_id=1, source_target_pairs={{0,2},{1,3},{2,4},{3,5},{4,6},{5,7},{6,0},{7,1},{8,10},{9,11},{10,... | collective-permute-start | bytes 786440 | tf_op jit(solution)/shard_map/ppermute | solution.py:112
  32.3 21.0 %collective-permute-start.3 = (bf16[64,2048]{1,0:T(8,128)(2,1)S(1)}, bf16[64,2048]{1,0:T(8,128)(2,1)S(1)}, u32[]{:S(2)}, u32[]{:S(2)}) collective-permute-start(bf16[64,2048]{1,0:T(8,128)(2,1)S(1)} %get-tuple-element.13), channel_id=1, source_target_pairs={{0,4},{1,5},{2,6},{3,7},{4,0},{5,1},{6,2},{7,3},{8,12},{9,13},{10,... | collective-permute-start | bytes 786440 | tf_op jit(solution)/shard_map/ppermute | solution.py:112
  36.7 16.6 %collective-permute-start.4 = (bf16[64,2048]{1,0:T(8,128)(2,1)S(1)}, bf16[64,2048]{1,0:T(8,128)(2,1)S(1)}, u32[]{:S(2)}, u32[]{:S(2)}) collective-permute-start(bf16[64,2048]{1,0:T(8,128)(2,1)S(1)} %get-tuple-element.14), channel_id=1, source_target_pairs={{0,6},{1,7},{2,0},{3,1},{4,2},{5,3},{6,4},{7,5},{8,14},{9,15},{10,... | collective-permute-start | bytes 786440 | tf_op jit(solution)/shard_map/ppermute | solution.py:112
  41.5 21.9 %all-to-all-start.1 = ((bf16[64,5,2,128]{3,2,1,0:T(2,128)(2,1)}), bf16[64,5,2,128]{3,2,1,0:T(2,128)(2,1)}, u32[]{:S(2)}, u32[]{:S(2)}) async-start(bf16[64,5,2,128]{3,2,1,0:T(2,128)(2,1)} %chunk_sum.1), calls=%async_computation.1 | async-start | bytes 327680 | tf_op jit(solution)/shard_map/all_to_all | solution.py:120
  53.5 14.1 %collective-permute-start.5 = (bf16[32,2048]{1,0:T(8,128)(2,1)S(1)}, bf16[32,2048]{1,0:T(8,128)(2,1)S(1)}, u32[]{:S(2)}, u32[]{:S(2)}) collective-permute-start(bf16[32,2048]{1,0:T(8,128)(2,1)S(1)} %split.15), channel_id=1, source_target_pairs={{0,1},{1,0},{2,3},{3,2},{4,5},{5,4},{6,7},{7,6},{8,9},{9,8},{10,11... | collective-permute-start | bytes 393224 | tf_op jit(solution)/shard_map/ppermute | solution.py:126

commit v4 on v3

v4 whole, which is shorter than its diff:
```python
import functools
import math

import jax
import jax.numpy as jnp
from jax import lax
from jax.experimental import pallas as pl
from jax.experimental.pallas import tpu as pltpu
from jax.sharding import PartitionSpec as P

COLS = 1024
VMEM = pl.BlockSpec(memory_space=pltpu.VMEM)
SMEM = pl.BlockSpec(memory_space=pltpu.SMEM)


def cost(flops):
    return pl.CostEstimate(flops=flops, bytes_accessed=1 << 20, transcendentals=0)


def halo_rows(array):
    size = lax.axis_size("space")
    up = [(i, i + 1) for i in range(size - 1)]
    down = [(j, i) for i, j in up]
    before = lax.ppermute(array[:, -COLS:], "space", up)
    after = lax.ppermute(array[:, :COLS], "space", down)
    return before, after


def put_line(stack_ref, line, at):
    filters, cols = line.shape
    column = lax.broadcasted_iota(jnp.int32, (filters, cols), 1)
    wide = line.astype(jnp.float32)
    left = jnp.where(column == cols - 1, 0.0, pltpu.roll(wide, cols - 1, 1)).astype(line.dtype)
    right = jnp.where(column == 0, 0.0, pltpu.roll(wide, 1, 1)).astype(line.dtype)
    for i in range(3):
        pixel_row = at - (2 - i)
        if 0 <= pixel_row < 2:
            for j, moved in enumerate((left, line, right)):
                top = (3 * i + j) * filters
                stack_ref[top:top + filters, pixel_row * cols:(pixel_row + 1) * cols] = moved


def inner_kernel(grad_ref, acts_ref, stack_ref, held_ref, sem):
    copy = pltpu.make_async_copy(acts_ref, held_ref, sem)
    copy.start()
    put_line(stack_ref, grad_ref[:, :COLS], 1)
    put_line(stack_ref, grad_ref[:, COLS:], 2)
    edge = jnp.zeros((3 * grad_ref.shape[0], COLS), stack_ref.dtype)
    stack_ref[0:edge.shape[0], COLS:] = edge
    stack_ref[2 * edge.shape[0]:, :COLS] = edge
    copy.wait()


def outer_kernel(scale, before_ref, after_ref, acts_ref, inner_ref, stack_ref, chunk_ref):
    put_line(stack_ref, before_ref[...], 0)
    put_line(stack_ref, after_ref[...], 3)
    terms = lax.dot_general(stack_ref[...], acts_ref[...], (((1,), (1,)), ((), ())), preferred_element_type=jnp.float32)
    terms = (terms * scale).astype(chunk_ref.dtype)
    for t in range(72):
        row, col = t // 2 * 8, t % 2 * 128
        chunk_ref[t] = terms[row:row + 8, col:col + 128]
    chunk_ref[72:80] = jnp.zeros((8, 8, 128), chunk_ref.dtype)


def parts_kernel(n_x, share, where_ref, taps_ref, stack_ref, *rest):
    outs, turned, order = rest[:n_x], rest[n_x], rest[n_x + 1]
    turned[...] = taps_ref[...].astype(jnp.float32).T.astype(jnp.bfloat16)
    here, half = where_ref[0], where_ref[1]
    for k in range(n_x):
        block = lax.rem(here + k, n_x) * 2
        for h in range(2):
            start = pl.multiple_of((block + lax.rem(half + h, 2)) * share, share)
            order[(2 * k + h) * share:(2 * k + h + 1) * share, :] = turned[pl.ds(start, share), :]
    wide = 512
    for c in range(stack_ref.shape[1] // wide):
        cols = slice(c * wide, c * wide + wide)
        got = jnp.dot(order[...], stack_ref[:, cols], preferred_element_type=jnp.float32).astype(jnp.bfloat16)
        for k in range(n_x):
            outs[k][:, cols] = got[2 * k * share:2 * (k + 1) * share, :]


def body(activations, out_grad, kernel):
    channels, pixels = activations.shape
    filters = out_grad.shape[0]
    n_space = lax.axis_size("space")
    n_filt = lax.axis_size("filt")
    n_x = n_filt // 2
    share = channels // n_filt
    scale = 1.0 / math.sqrt(pixels * n_space)
    before, after = halo_rows(out_grad)
    me = lax.axis_index("filt")
    where = jnp.stack([me // 2, me % 2])

    stack_type = jax.ShapeDtypeStruct((9 * filters, pixels), jnp.bfloat16)
    inner, held = pl.pallas_call(
        inner_kernel,
        out_shape=[stack_type, jax.ShapeDtypeStruct(activations.shape, activations.dtype)],
        in_specs=[VMEM, pl.BlockSpec(memory_space=pl.ANY)], out_specs=[VMEM, VMEM],
        scratch_shapes=[pltpu.SemaphoreType.DMA],
        cost_estimate=cost(4_000_000_000),
        compiler_params=pltpu.CompilerParams(vmem_limit_bytes=32 << 20),
        name="inner",
    )(out_grad, activations)
    stack, chunks = pl.pallas_call(
        functools.partial(outer_kernel, scale),
        out_shape=[stack_type, jax.ShapeDtypeStruct((80, 8, 128), jnp.bfloat16)],
        in_specs=[VMEM] * 4, out_specs=[VMEM] * 2, cost_estimate=cost(1_000_000_000),
        input_output_aliases={3: 0},
        compiler_params=pltpu.CompilerParams(vmem_limit_bytes=32 << 20),
        name="outer",
    )(before, after, held, inner)
    got = lax.all_to_all(chunks.reshape(64, 5, 2, 128), "space", 0, 0, tiled=True).reshape(chunks.shape)

    taps = kernel.transpose(1, 2, 0, 3).reshape(9 * filters, channels)
    part = jax.ShapeDtypeStruct((2 * share, pixels), jnp.bfloat16)
    own, *parts = pl.pallas_call(
        functools.partial(parts_kernel, n_x, share),
        out_shape=[part] * n_x,
        in_specs=[SMEM, VMEM, VMEM],
        out_specs=[VMEM] * n_x,
        scratch_shapes=[pltpu.VMEM((channels, 9 * filters), jnp.bfloat16)] * 2,
        cost_estimate=cost(P_COST),
        compiler_params=pltpu.CompilerParams(vmem_limit_bytes=32 << 20),
        name="parts",
    )(where, taps, stack)
    arrived = []
    for k in range(1, n_x):
        pairs = [(i, (i + 2 * k) % n_filt) for i in range(n_filt)]
        arrived.append(lax.ppermute(parts[k - 1], "filt", pairs))

    four = jnp.sum(got.reshape(16, 40, 128).astype(jnp.float32), axis=0)
    total = ((four[0:10] + four[10:20]) + (four[20:30] + four[30:40])).astype(jnp.bfloat16)
    everyone = jnp.broadcast_to(jnp.concatenate([total] * 4, axis=0)[None], (16, 40, 128))
    own, everyone = lax.optimization_barrier((own, everyone))
    full = lax.all_to_all(everyone.reshape(64, 5, 2, 128), "space", 0, 0, tiled=True).reshape(chunks.shape)

    summed = own.astype(jnp.float32)
    for other in arrived:
        summed = summed + other.astype(jnp.float32)
    keep, give = jnp.split(summed, 2, axis=0)
    swapped = lax.ppermute(give.astype(jnp.bfloat16), "filt", [(i, i ^ 1) for i in range(n_filt)])
    weight = full[:72].reshape(36, 2, 8, 128).transpose(0, 2, 1, 3).reshape(9 * filters, channels).astype(jnp.float32)
    swapped, weight = lax.optimization_barrier((swapped, weight))
    input_grad = (keep + swapped.astype(jnp.float32)).astype(jnp.bfloat16)

    weight_grad = weight.reshape(3, 3, filters, channels).transpose(2, 0, 1, 3)
    return (input_grad, weight_grad)


P_COST = 115_000_000_000


def solution(mesh):
    in_specs = (P(None, "space"), P("filt", "space"), P("filt", None, None, None))
    out_specs = (P("filt", "space"), P("filt", None, None, None))
    return jax.shard_map(body, mesh=mesh, in_specs=in_specs, out_specs=out_specs, check_vma=False)
```

time: 68.7 us -> 66 us (0.961)
  starting transfers between devices: 52.9 us -> 50.8 us
  Pallas kernels: 4.87 us -> 2.78 us
  waiting for transfers between devices: 4.46 us -> 5.64 us
  local copies, waits for them, and re-layouts: 2.71 us -> 3.73 us
    ppermute x1, starting transfers between devices: 5.49 us -> 8.79 us  [halo_rows(): after = lax.ppermute(array[:, :COLS], 'space', down)]
    ppermute x1, starting transfers between devices: 4.59 us -> 1.92 us  [halo_rows(): before = lax.ppermute(array[:, -COLS:], 'space', up)]
    all_to_all x2, starting transfers between devices: 24.3 us -> 21.7 us  [the longest x1 11.6 us: body(): lax.all_to_all(everyone.reshape(64, 5, 2, 128), 'space', 0, 0, tiled=True)]
    pallas_call x2, Pallas kernels: 3.52 us -> 1.43 us  [the longest x1 1.2 us: body(): pl.pallas_call(functools.partial(outer_kernel, scale), out_shape=[stack_t...]
    ppermute x1, waiting for transfers between devices: 2.42 us -> 3.54 us  [body(): lax.ppermute(give.astype(jnp.bfloat16), 'filt', [(i, i ^ 1) for i in rang...]
    concatenate x1, other arithmetic: 0.81 us -> 0.01 us  [body(): jnp.concatenate([total] * 4, axis=0)[None]]
    convert_element_type x0 -> x2, other arithmetic: none -> 0.74 us  [the longest x1 0.73 us: body(): full[:72].reshape(36, 2, 8, 128).transpose(0, 2, 1, 3)]
    broadcast_in_dim x0 -> x1, local copies, waits for them, and re-layouts: none -> 0.69 us  [body(): jnp.broadcast_to(jnp.concatenate([total] * 4, axis=0)[None], (16, 40, 128))]
  transfers between devices with their start and end apart: 8 -> 8, of which waited for: 2 -> 2; matrix products, arithmetic and copies ran while one was open for 2% -> 3% of each run, Pallas kernels for 7% -> 2%
where the time goes in v4:
time: 66 us; the launch traced here: 65.5 us
  starting transfers between devices  50.8 us (77%)
  waiting for transfers between devices  5.64 us (9%)
  local copies, waits for them, and re-layouts  3.73 us (6%)
  Pallas kernels  2.78 us (4%)
  other arithmetic  1.67 us (3%)
  between operations  0.84 us (1%)
    all_to_all x1, starting transfers between devices, body(): lax.all_to_all(everyone.reshape(64, 5, 2, 128), 'space', 0, 0, tiled=True)  11.6 us
    ppermute x3, starting transfers between devices, body(): arrived.append(lax.ppermute(parts[k - 1], 'filt', pairs))  10.5 us
    all_to_all x1, starting transfers between devices, body(): lax.all_to_all(chunks.reshape(64, 5, 2, 128), 'space', 0, 0, tiled=True)  10.1 us
    ppermute x1, starting transfers between devices, halo_rows(): after = lax.ppermute(array[:, :COLS], 'space', down)  8.79 us
    ppermute x1, starting transfers between devices, body(): lax.ppermute(give.astype(jnp.bfloat16), 'filt', [(i, i ^ 1) for i in rang...  7.94 us
    ppermute x1, waiting for transfers between devices, body(): lax.ppermute(give.astype(jnp.bfloat16), 'filt', [(i, i ^ 1) for i in rang...  3.54 us
    unnamed x6, local copies, waits for them, and re-layouts  2.13 us
    all_to_all x1, waiting for transfers between devices, body(): lax.all_to_all(everyone.reshape(64, 5, 2, 128), 'space', 0, 0, tiled=True)  2.08 us
  transfers between devices with their start and end apart: 8, of which 2 were waited for; matrix products, arithmetic and copies ran while one was open for 3% of the time, Pallas kernels for 2%

profile of v4, /device:TPU:1, one launch (start us, length us, event | category | flops | bytes accessed | tf_op | source)
XLA Modules:
  0.0 65.5 jit_solution(3833720055054402708)
XLA Ops:
  0.6 0.9 %fusion.3 = (bf16[32,1024]{1,0:T(8,128)(2,1)S(1)}, bf16[32,1024]{1,0:T(8,128)(2,1)S(1)}) fusion(bf16[32,2048]{1,0:T(8,128)(2,1)} %grad_ref.1), kind=kLoop, calls=%fused_computation.12 | loop fusion | bytes 262144 | tf_op jit(solution)/shard_map/slice | solution.py:25
  1.5 8.8 %collective-permute-start.1 = (bf16[32,1024]{1,0:T(8,128)(2,1)S(1)}, bf16[32,1024]{1,0:T(8,128)(2,1)S(1)}, u32[]{:S(2)}, u32[]{:S(2)}) collective-permute-start(bf16[32,1024]{1,0:T(8,128)(2,1)S(1)} %get-tuple-element.26), channel_id=1, source_target_pairs={{8,0},{16,8},{24,16},{32,24},{40,32},{48,40},{56,48},{64,56},{72,6... | collective-permute-start | bytes 196616 | tf_op jit(solution)/shard_map/ppermute | solution.py:25
  10.3 1.9 %collective-permute-start = (bf16[32,1024]{1,0:T(8,128)(2,1)S(1)}, bf16[32,1024]{1,0:T(8,128)(2,1)S(1)}, u32[]{:S(2)}, u32[]{:S(2)}) collective-permute-start(bf16[32,1024]{1,0:T(8,128)(2,1)S(1)} %get-tuple-element.27), channel_id=1, source_target_pairs={{0,8},{8,16},{16,24},{24,32},{32,40},{40,48},{48,56},{56,64},{64,7... | collective-permute-start | bytes 196616 | tf_op jit(solution)/shard_map/ppermute | solution.py:24
  12.3 0.0 copy-start
  12.3 0.9 %copy-done = bf16[32,2048]{1,0:T(8,128)(2,1)S(1)} copy-done((bf16[32,2048]{1,0:T(8,128)(2,1)S(1)}, bf16[32,2048]{1,0:T(8,128)(2,1)}, u32[]{:S(2)}) %copy-start) | copy-done | bytes 131096
  13.2 1.2 %copy-done.1 = bf16[256,2048]{1,0:T(8,128)(2,1)S(1)} copy-done((bf16[256,2048]{1,0:T(8,128)(2,1)S(1)}, bf16[256,2048]{1,0:T(8,128)(2,1)}, u32[]{:S(2)}) %copy-start.1) | copy-done | bytes 1048600
  14.4 0.2 inner.1
  14.6 0.1 pad_add_fusion.where_ref
  14.7 1.2 %outer.1 = (bf16[288,2048]{1,0:T(8,128)(2,1)S(1)}, bf16[80,8,128]{2,1,0:T(8,128)(2,1)}) custom-call(bf16[32,1024]{1,0:T(8,128)(2,1)S(1)} %collective-permute-done.before_ref, bf16[32,1024]{1,0:T(8,128)(2,1)S(1)} %collective-permute-done.1.after_ref, bf16[256,2048]{1,0:T(8,128)(2,1)S(1)} %get-tuple-element.14.acts_ref, ...), custom_call_target="tpu_custom_call", output_to_operand_aliasing={{0}: (3, {})} | custom-call | flops 1000000000 | bytes 1048576 | tf_op jit(solution)/shard_map/outer/pallas_call | solution.py:104
  15.9 10.1 %all-to-all-start = ((bf16[64,5,2,128]{3,2,1,0:T(2,128)(2,1)}), bf16[64,5,2,128]{3,2,1,0:T(2,128)(2,1)S(1)}, u32[]{:S(2)}, u32[]{:S(2)}) async-start(bf16[64,5,2,128]{3,2,1,0:T(2,128)(2,1)} %bitcast.4), calls=%async_computation | async-start | bytes 327680 | tf_op jit(solution)/shard_map/all_to_all | solution.py:112
  26.0 1.4 %parts.1 = (bf16[64,2048]{1,0:T(8,128)(2,1)S(1)}, bf16[64,2048]{1,0:T(8,128)(2,1)S(1)}, bf16[64,2048]{1,0:T(8,128)(2,1)S(1)}, bf16[64,2048]{1,0:T(8,128)(2,1)S(1)}) custom-call(s32[2]{0:T(128)S(1)} %pad_add_fusion.where_ref, bf16[288,256]{1,0:T(8,128)(2,1)S(1)} %bitcast.19, bf16[288,2048]{1,0:T(8,128)(2,1)S(1)} %get-tuple-element.16.stack_ref), custom_call_target="tpu_custom_call" | custom-call | flops 115000000512 | bytes 1048576 | tf_op jit(solution)/shard_map/parts/pallas_call | solution.py:116
  27.4 3.1 %collective-permute-start.2 = (bf16[64,2048]{1,0:T(8,128)(2,1)S(1)}, bf16[64,2048]{1,0:T(8,128)(2,1)S(1)}, u32[]{:S(2)}, u32[]{:S(2)}) collective-permute-start(bf16[64,2048]{1,0:T(8,128)(2,1)S(1)} %get-tuple-element.20), channel_id=1, source_target_pairs={{0,2},{1,3},{2,4},{3,5},{4,6},{5,7},{6,0},{7,1},{8,10},{9,11},{10,... | collective-permute-start | bytes 786440 | tf_op jit(solution)/shard_map/ppermute | solution.py:129
  30.5 4.4 %collective-permute-start.3 = (bf16[64,2048]{1,0:T(8,128)(2,1)S(1)}, bf16[64,2048]{1,0:T(8,128)(2,1)S(1)}, u32[]{:S(2)}, u32[]{:S(2)}) collective-permute-start(bf16[64,2048]{1,0:T(8,128)(2,1)S(1)} %get-tuple-element.21), channel_id=1, source_target_pairs={{0,4},{1,5},{2,6},{3,7},{4,0},{5,1},{6,2},{7,3},{8,12},{9,13},{10,... | collective-permute-start | bytes 786440 | tf_op jit(solution)/shard_map/ppermute | solution.py:129
  34.9 3.1 %collective-permute-start.4 = (bf16[64,2048]{1,0:T(8,128)(2,1)S(1)}, bf16[64,2048]{1,0:T(8,128)(2,1)S(1)}, u32[]{:S(2)}, u32[]{:S(2)}) collective-permute-start(bf16[64,2048]{1,0:T(8,128)(2,1)S(1)} %get-tuple-element.22), channel_id=1, source_target_pairs={{0,6},{1,7},{2,0},{3,1},{4,2},{5,3},{6,4},{7,5},{8,14},{9,15},{10,... | collective-permute-start | bytes 786440 | tf_op jit(solution)/shard_map/ppermute | solution.py:129
  38.0 0.0 all-to-all-done
  38.0 0.7 %broadcast_in_dim.2 = bf16[16,40,128]{2,1,0:T(8,128)(2,1)} broadcast(bf16[40,128]{1,0:T(8,128)(2,1)S(1)} %pad_maximum_fusion), dimensions={1,2} | broadcast | bytes 174080 | tf_op jit(solution)/shard_map/broadcast_in_dim | solution.py:133
  38.7 11.6 %all-to-all-start.1 = ((bf16[64,5,2,128]{3,2,1,0:T(2,128)(2,1)}), bf16[64,5,2,128]{3,2,1,0:T(2,128)(2,1)S(1)}, u32[]{:S(2)}, u32[]{:S(2)}) async-start(bf16[64,5,2,128]{3,2,1,0:T(2,128)(2,1)} %bitcast.6), calls=%async_computation.1 | async-start | bytes 327680 | tf_op jit(solution)/shard_map/all_to_all | solution.py:135
  50.3 0.0 collective-permute-done.2
  50.3 0.1 convert_add_fusion
  50.5 7.9 %collective-permute-start.5 = (bf16[32,2048]{1,0:T(8,128)(2,1)S(1)}, bf16[32,2048]{1,0:T(8,128)(2,1)S(1)}, u32[]{:S(2)}, u32[]{:S(2)}) collective-permute-start(bf16[32,2048]{1,0:T(8,128)(2,1)S(1)} %split.15), channel_id=1, source_target_pairs={{0,1},{1,0},{2,3},{3,2},{4,5},{5,4},{6,7},{7,6},{8,9},{9,8},{10,11... | collective-permute-start | bytes 393224 | tf_op jit(solution)/shard_map/ppermute | solution.py:141
  58.4 2.1 %all-to-all-done.1 = bf16[64,5,2,128]{3,2,1,0:T(2,128)(2,1)S(1)} async-done(((bf16[64,5,2,128]{3,2,1,0:T(2,128)(2,1)}), bf16[64,5,2,128]{3,2,1,0:T(2,128)(2,1)S(1)}, u32[]{:S(2)}, u32[]{:S(2)}) %all-to-all-start.1) | async-done | bytes 163872 | tf_op jit(solution)/shard_map/all_to_all | solution.py:135
  60.5 0.7 %convert_bitcast_fusion = f32[288,256]{1,0:T(8,128)} fusion(bf16[36,2,8,128]{3,2,1,0:T(8,128)(2,1)S(1)} %bitcast.22), kind=kLoop, calls=%fused_computation.2 | loop fusion | flops 73728 | bytes 442368 | tf_op jit(solution)/shard_map/convert_element_type | solution.py:142
  61.3 3.5 %collective-permute-done.5 = bf16[32,2048]{1,0:T(8,128)(2,1)S(1)} collective-permute-done((bf16[32,2048]{1,0:T(8,128)(2,1)S(1)}, bf16[32,2048]{1,0:T(8,128)(2,1)S(1)}, u32[]{:S(2)}, u32[]{:S(2)}) %collective-permute-start.5) | collective-permute-done | bytes 131104 | tf_op jit(solution)/shard_map/ppermute | solution.py:141
  64.8 0.7 %fusion = bf16[32,2048]{1,0:T(8,128)(2,1)} fusion(f32[64,2048]{1,0:T(8,128)S(1)} %convert_add_fusion, bf16[32,2048]{1,0:T(8,128)(2,1)S(1)} %collective-permute-done.5), kind=kLoop, calls=%fused_computation.5 | loop fusion | flops 196608 | bytes 524288 | tf_op jit(solution)/shard_map/convert_element_type | solution.py:144
  (12 shorter events, 0.1 us)
Async XLA Ops:
  1.5 13.2 %collective-permute-start.1 = (bf16[32,1024]{1,0:T(8,128)(2,1)S(1)}, bf16[32,1024]{1,0:T(8,128)(2,1)S(1)}, u32[]{:S(2)}, u32[]{:S(2)}) collective-permute-start(bf16[32,1024]{1,0:T(8,128)(2,1)S(1)} %get-tuple-element.26), channel_id=1, source_target_pairs={{8,0},{16,8},{24,16},{32,24},{40,32},{48,40},{56,48},{64,56},{72,6... | collective-permute-start | bytes 196616 | tf_op jit(solution)/shard_map/ppermute | solution.py:25
  10.3 4.4 %collective-permute-start = (bf16[32,1024]{1,0:T(8,128)(2,1)S(1)}, bf16[32,1024]{1,0:T(8,128)(2,1)S(1)}, u32[]{:S(2)}, u32[]{:S(2)}) collective-permute-start(bf16[32,1024]{1,0:T(8,128)(2,1)S(1)} %get-tuple-element.27), channel_id=1, source_target_pairs={{0,8},{8,16},{16,24},{24,32},{32,40},{40,48},{48,56},{56,64},{64,7... | collective-permute-start | bytes 196616 | tf_op jit(solution)/shard_map/ppermute | solution.py:24
  12.3 0.9 %copy-start = (bf16[32,2048]{1,0:T(8,128)(2,1)S(1)}, bf16[32,2048]{1,0:T(8,128)(2,1)}, u32[]{:S(2)}) copy-start(bf16[32,2048]{1,0:T(8,128)(2,1)} %grad_ref.1) | copy-start | bytes 393220
  13.2 1.2 %copy-start.1 = (bf16[256,2048]{1,0:T(8,128)(2,1)S(1)}, bf16[256,2048]{1,0:T(8,128)(2,1)}, u32[]{:S(2)}) copy-start(bf16[256,2048]{1,0:T(8,128)(2,1)} %acts_ref.1) | copy-start | bytes 3145732
  14.7 11.3 %copy-start.2 = (bf16[32,3,3,256]{3,0,2,1:T(8,128)(2,1)S(1)}, bf16[32,3,3,256]{3,0,2,1:T(8,128)(2,1)}, u32[]{:S(2)}) copy-start(bf16[32,3,3,256]{3,0,2,1:T(8,128)(2,1)} %param.5) | copy-start | bytes 442372
  15.9 22.0 %all-to-all-start = ((bf16[64,5,2,128]{3,2,1,0:T(2,128)(2,1)}), bf16[64,5,2,128]{3,2,1,0:T(2,128)(2,1)S(1)}, u32[]{:S(2)}, u32[]{:S(2)}) async-start(bf16[64,5,2,128]{3,2,1,0:T(2,128)(2,1)} %bitcast.4), calls=%async_computation | async-start | bytes 327680 | tf_op jit(solution)/shard_map/all_to_all | solution.py:112
  27.4 22.9 %collective-permute-start.2 = (bf16[64,2048]{1,0:T(8,128)(2,1)S(1)}, bf16[64,2048]{1,0:T(8,128)(2,1)S(1)}, u32[]{:S(2)}, u32[]{:S(2)}) collective-permute-start(bf16[64,2048]{1,0:T(8,128)(2,1)S(1)} %get-tuple-element.20), channel_id=1, source_target_pairs={{0,2},{1,3},{2,4},{3,5},{4,6},{5,7},{6,0},{7,1},{8,10},{9,11},{10,... | collective-permute-start | bytes 786440 | tf_op jit(solution)/shard_map/ppermute | solution.py:129
  30.5 19.8 %collective-permute-start.3 = (bf16[64,2048]{1,0:T(8,128)(2,1)S(1)}, bf16[64,2048]{1,0:T(8,128)(2,1)S(1)}, u32[]{:S(2)}, u32[]{:S(2)}) collective-permute-start(bf16[64,2048]{1,0:T(8,128)(2,1)S(1)} %get-tuple-element.21), channel_id=1, source_target_pairs={{0,4},{1,5},{2,6},{3,7},{4,0},{5,1},{6,2},{7,3},{8,12},{9,13},{10,... | collective-permute-start | bytes 786440 | tf_op jit(solution)/shard_map/ppermute | solution.py:129
  34.9 15.4 %collective-permute-start.4 = (bf16[64,2048]{1,0:T(8,128)(2,1)S(1)}, bf16[64,2048]{1,0:T(8,128)(2,1)S(1)}, u32[]{:S(2)}, u32[]{:S(2)}) collective-permute-start(bf16[64,2048]{1,0:T(8,128)(2,1)S(1)} %get-tuple-element.22), channel_id=1, source_target_pairs={{0,6},{1,7},{2,0},{3,1},{4,2},{5,3},{6,4},{7,5},{8,14},{9,15},{10,... | collective-permute-start | bytes 786440 | tf_op jit(solution)/shard_map/ppermute | solution.py:129
  38.7 21.8 %all-to-all-start.1 = ((bf16[64,5,2,128]{3,2,1,0:T(2,128)(2,1)}), bf16[64,5,2,128]{3,2,1,0:T(2,128)(2,1)S(1)}, u32[]{:S(2)}, u32[]{:S(2)}) async-start(bf16[64,5,2,128]{3,2,1,0:T(2,128)(2,1)} %bitcast.6), calls=%async_computation.1 | async-start | bytes 327680 | tf_op jit(solution)/shard_map/all_to_all | solution.py:135
  50.5 14.3 %collective-permute-start.5 = (bf16[32,2048]{1,0:T(8,128)(2,1)S(1)}, bf16[32,2048]{1,0:T(8,128)(2,1)S(1)}, u32[]{:S(2)}, u32[]{:S(2)}) collective-permute-start(bf16[32,2048]{1,0:T(8,128)(2,1)S(1)} %split.15), channel_id=1, source_target_pairs={{0,1},{1,0},{2,3},{3,2},{4,5},{5,4},{6,7},{7,6},{8,9},{9,8},{10,11... | collective-permute-start | bytes 393224 | tf_op jit(solution)/shard_map/ppermute | solution.py:141

commit v5 on v4

--- a/solution.py
+++ b/solution.py
@@ -17,13 +17,10 @@
     return pl.CostEstimate(flops=flops, bytes_accessed=1 << 20, transcendentals=0)
 
 
-def halo_rows(array):
+def halo_rows(far, near):
     size = lax.axis_size("space")
-    up = [(i, i + 1) for i in range(size - 1)]
-    down = [(j, i) for i, j in up]
-    before = lax.ppermute(array[:, -COLS:], "space", up)
-    after = lax.ppermute(array[:, :COLS], "space", down)
-    return before, after
+    across = [(i, i + 1) for i in range(1, size - 1, 2)] + [(i + 1, i) for i in range(1, size - 1, 2)]
+    return lax.ppermute(far, "space", across), lax.ppermute(near, "space", [(i, i ^ 1) for i in range(size)])
 
 
 def put_line(stack_ref, line, at):
@@ -40,20 +37,24 @@
                 stack_ref[top:top + filters, pixel_row * cols:(pixel_row + 1) * cols] = moved
 
 
-def inner_kernel(grad_ref, acts_ref, stack_ref, held_ref, sem):
-    copy = pltpu.make_async_copy(acts_ref, held_ref, sem)
-    copy.start()
+def line_kernel(core_ref, grad_ref, far_ref):
+    far_ref[...] = grad_ref[:, pl.ds(pl.multiple_of(core_ref[0] * COLS, COLS), COLS)]
+
+
+def inner_kernel(core_ref, grad_ref, near_ref, stack_ref):
+    near_ref[...] = grad_ref[:, pl.ds(pl.multiple_of((1 - core_ref[0]) * COLS, COLS), COLS)]
     put_line(stack_ref, grad_ref[:, :COLS], 1)
     put_line(stack_ref, grad_ref[:, COLS:], 2)
     edge = jnp.zeros((3 * grad_ref.shape[0], COLS), stack_ref.dtype)
     stack_ref[0:edge.shape[0], COLS:] = edge
     stack_ref[2 * edge.shape[0]:, :COLS] = edge
-    copy.wait()
 
 
-def outer_kernel(scale, before_ref, after_ref, acts_ref, inner_ref, stack_ref, chunk_ref):
-    put_line(stack_ref, before_ref[...], 0)
-    put_line(stack_ref, after_ref[...], 3)
+def outer_kernel(scale, core_ref, far_ref, near_ref, acts_ref, inner_ref, stack_ref, chunk_ref):
+    far, near = far_ref[...].astype(jnp.float32), near_ref[...].astype(jnp.float32)
+    first_core = core_ref[0] == 0
+    put_line(stack_ref, jnp.where(first_core, far, near).astype(far_ref.dtype), 0)
+    put_line(stack_ref, jnp.where(first_core, near, far).astype(far_ref.dtype), 3)
     terms = lax.dot_general(stack_ref[...], acts_ref[...], (((1,), (1,)), ((), ())), preferred_element_type=jnp.float32)
     terms = (terms * scale).astype(chunk_ref.dtype)
     for t in range(72):
@@ -87,28 +88,30 @@
     n_x = n_filt // 2
     share = channels // n_filt
     scale = 1.0 / math.sqrt(pixels * n_space)
-    before, after = halo_rows(out_grad)
+    line_type = jax.ShapeDtypeStruct((filters, COLS), out_grad.dtype)
+    core = (lax.axis_index("space") % 2).reshape(1)
+    far = pl.pallas_call(
+        line_kernel, out_shape=line_type, in_specs=[SMEM, VMEM], out_specs=VMEM, cost_estimate=cost(L_COST),
+        compiler_params=pltpu.CompilerParams(vmem_limit_bytes=32 << 20), name="line",
+    )(core, out_grad)
     me = lax.axis_index("filt")
     where = jnp.stack([me // 2, me % 2])
 
     stack_type = jax.ShapeDtypeStruct((9 * filters, pixels), jnp.bfloat16)
-    inner, held = pl.pallas_call(
-        inner_kernel,
-        out_shape=[stack_type, jax.ShapeDtypeStruct(activations.shape, activations.dtype)],
-        in_specs=[VMEM, pl.BlockSpec(memory_space=pl.ANY)], out_specs=[VMEM, VMEM],
-        scratch_shapes=[pltpu.SemaphoreType.DMA],
-        cost_estimate=cost(4_000_000_000),
+    near, inner = pl.pallas_call(
+        inner_kernel, out_shape=[line_type, stack_type], in_specs=[SMEM, VMEM], out_specs=[VMEM] * 2,
+        cost_estimate=cost(1_000_000), name="inner",
         compiler_params=pltpu.CompilerParams(vmem_limit_bytes=32 << 20),
-        name="inner",
-    )(out_grad, activations)
+    )(core, out_grad)
+    far, near = halo_rows(far, near)
     stack, chunks = pl.pallas_call(
         functools.partial(outer_kernel, scale),
         out_shape=[stack_type, jax.ShapeDtypeStruct((80, 8, 128), jnp.bfloat16)],
-        in_specs=[VMEM] * 4, out_specs=[VMEM] * 2, cost_estimate=cost(1_000_000_000),
-        input_output_aliases={3: 0},
+        in_specs=[SMEM] + [VMEM] * 4, out_specs=[VMEM] * 2, cost_estimate=cost(1_000_000_000),
+        input_output_aliases={4: 0},
         compiler_params=pltpu.CompilerParams(vmem_limit_bytes=32 << 20),
         name="outer",
-    )(before, after, held, inner)
+    )(core, far, near, activations, inner)
     got = lax.all_to_all(chunks.reshape(64, 5, 2, 128), "space", 0, 0, tiled=True).reshape(chunks.shape)
 
     taps = kernel.transpose(1, 2, 0, 3).reshape(9 * filters, channels)
@@ -148,6 +151,7 @@
 
 
 P_COST = 115_000_000_000
+L_COST = 115_000_000_000
 
 
 def solution(mesh):

time: 66 us -> 64.1 us (0.971)
  local copies, waits for them, and re-layouts: 3.73 us -> 1.62 us
  waiting for transfers between devices: 5.64 us -> 6.42 us
    unnamed x6, local copies, waits for them, and re-layouts: 2.13 us -> 0.9 us
    ppermute x2, starting transfers between devices: 10.7 us -> 9.58 us  [the longest x1 4.86 us: halo_rows(): lax.ppermute(near, 'space', [(i, i ^ 1) for i in range(size)])]
    slice x1 -> x0, local copies, waits for them, and re-layouts: 0.88 us -> none  [halo_rows(): after = lax.ppermute(array[:, :COLS], 'space', down)]
    all_to_all x1, starting transfers between devices: 10.1 us -> 10.9 us  [body(): lax.all_to_all(chunks.reshape(64, 5, 2, 128), 'space', 0, 0, tiled=True)]
    ppermute x2, waiting for transfers between devices: 0.01 us -> 0.79 us  [the longest x1 0.78 us: halo_rows(): lax.ppermute(near, 'space', [(i, i ^ 1) for i in range(size)])]
  transfers between devices with their start and end apart: 8 -> 8, of which waited for: 2 -> 3; matrix products, arithmetic and copies ran while one was open for 3% -> 3% of each run, Pallas kernels for 2% -> 2%
where the time goes in v5:
time: 64.1 us; the launch traced here: 63.7 us
  starting transfers between devices  50.5 us (79%)
  waiting for transfers between devices  6.42 us (10%)
  Pallas kernels  2.68 us (4%)
  other arithmetic  1.67 us (3%)
  local copies, waits for them, and re-layouts  1.62 us (3%)
  between operations  0.83 us (1%)
    all_to_all x1, starting transfers between devices, body(): lax.all_to_all(everyone.reshape(64, 5, 2, 128), 'space', 0, 0, tiled=True)  11.6 us
    all_to_all x1, starting transfers between devices, body(): lax.all_to_all(chunks.reshape(64, 5, 2, 128), 'space', 0, 0, tiled=True)  10.9 us
    ppermute x3, starting transfers between devices, body(): arrived.append(lax.ppermute(parts[k - 1], 'filt', pairs))  10.5 us
    ppermute x1, starting transfers between devices, body(): lax.ppermute(give.astype(jnp.bfloat16), 'filt', [(i, i ^ 1) for i in rang...  7.94 us
    ppermute x1, starting transfers between devices, halo_rows(): lax.ppermute(near, 'space', [(i, i ^ 1) for i in range(size)])  4.86 us
    ppermute x1, starting transfers between devices, halo_rows(): lax.ppermute(far, 'space', across)  4.72 us
    ppermute x1, waiting for transfers between devices, body(): lax.ppermute(give.astype(jnp.bfloat16), 'filt', [(i, i ^ 1) for i in rang...  3.54 us
    all_to_all x1, waiting for transfers between devices, body(): lax.all_to_all(everyone.reshape(64, 5, 2, 128), 'space', 0, 0, tiled=True)  2.08 us
  transfers between devices with their start and end apart: 8, of which 3 were waited for; matrix products, arithmetic and copies ran while one was open for 3% of the time, Pallas kernels for 2%

profile of v5, /device:TPU:1, one launch (start us, length us, event | category | flops | bytes accessed | tf_op | source)
XLA Modules:
  0.0 63.7 jit_solution(15897912995205680131)
XLA Ops:
  0.7 0.9 %copy-done = bf16[32,2048]{1,0:T(8,128)(2,1)S(1)} copy-done((bf16[32,2048]{1,0:T(8,128)(2,1)S(1)}, bf16[32,2048]{1,0:T(8,128)(2,1)}, u32[]{:S(2)}) %copy-start) | copy-done | bytes 131096
  1.6 4.7 %collective-permute-start = (bf16[32,1024]{1,0:T(8,128)(2,1)S(1)}, bf16[32,1024]{1,0:T(8,128)(2,1)S(1)}, u32[]{:S(2)}, u32[]{:S(2)}) collective-permute-start(bf16[32,1024]{1,0:T(8,128)(2,1)S(1)} %line.1), channel_id=1, source_target_pairs={{8,16},{24,32},{40,48},{56,64},{72,80},{88,96},{104,112},{120,128}... | collective-permute-start | bytes 196616 | tf_op jit(solution)/shard_map/ppermute | solution.py:23
  6.3 0.1 inner.1
  6.4 4.9 %collective-permute-start.1 = (bf16[32,1024]{1,0:T(8,128)(2,1)S(1)}, bf16[32,1024]{1,0:T(8,128)(2,1)S(1)}, u32[]{:S(2)}, u32[]{:S(2)}) collective-permute-start(bf16[32,1024]{1,0:T(8,128)(2,1)S(1)} %get-tuple-element.14), channel_id=1, source_target_pairs={{0,8},{8,0},{16,24},{24,16},{32,40},{40,32},{48,56},{56,48},{64,72... | collective-permute-start | bytes 196616 | tf_op jit(solution)/shard_map/ppermute | solution.py:23
  11.3 0.1 pad_add_fusion.where_ref
  11.4 0.0 collective-permute-done.far_ref
  11.4 0.8 %collective-permute-done.1.near_ref = bf16[32,1024]{1,0:T(8,128)(2,1)S(1)} collective-permute-done((bf16[32,1024]{1,0:T(8,128)(2,1)S(1)}, bf16[32,1024]{1,0:T(8,128)(2,1)S(1)}, u32[]{:S(2)}, u32[]{:S(2)}) %collective-permute-start.1) | collective-permute-done | bytes 65568 | tf_op jit(solution)/shard_map/ppermute | solution.py:23
  12.2 1.2 %outer.1 = (bf16[288,2048]{1,0:T(8,128)(2,1)S(1)}, bf16[80,8,128]{2,1,0:T(8,128)(2,1)}) custom-call(s32[1]{0:T(128)} %bitcast.4.core_ref, bf16[32,1024]{1,0:T(8,128)(2,1)S(1)} %collective-permute-done.far_ref, bf16[32,1024]{1,0:T(8,128)(2,1)S(1)} %collective-permute-done.1.near_ref, ...), custom_call_target="tpu_custom_call", output_to_operand_aliasing={{0}: (4, {})} | custom-call | flops 1000000000 | bytes 1048576 | tf_op jit(solution)/shard_map/outer/pallas_call | solution.py:107
  13.4 10.9 %all-to-all-start = ((bf16[64,5,2,128]{3,2,1,0:T(2,128)(2,1)}), bf16[64,5,2,128]{3,2,1,0:T(2,128)(2,1)S(1)}, u32[]{:S(2)}, u32[]{:S(2)}) async-start(bf16[64,5,2,128]{3,2,1,0:T(2,128)(2,1)} %bitcast.5), calls=%async_computation | async-start | bytes 327680 | tf_op jit(solution)/shard_map/all_to_all | solution.py:115
  24.3 1.3 %parts.1 = (bf16[64,2048]{1,0:T(8,128)(2,1)S(1)}, bf16[64,2048]{1,0:T(8,128)(2,1)S(1)}, bf16[64,2048]{1,0:T(8,128)(2,1)S(1)}, bf16[64,2048]{1,0:T(8,128)(2,1)S(1)}) custom-call(s32[2]{0:T(128)S(1)} %pad_add_fusion.where_ref, bf16[288,256]{1,0:T(8,128)(2,1)S(1)} %bitcast.20, bf16[288,2048]{1,0:T(8,128)(2,1)S(1)} %get-tuple-element.16.stack_ref), custom_call_target="tpu_custom_call" | custom-call | flops 115000000512 | bytes 1048576 | tf_op jit(solution)/shard_map/parts/pallas_call | solution.py:119
  25.6 3.1 %collective-permute-start.2 = (bf16[64,2048]{1,0:T(8,128)(2,1)S(1)}, bf16[64,2048]{1,0:T(8,128)(2,1)S(1)}, u32[]{:S(2)}, u32[]{:S(2)}) collective-permute-start(bf16[64,2048]{1,0:T(8,128)(2,1)S(1)} %get-tuple-element.20), channel_id=1, source_target_pairs={{0,2},{1,3},{2,4},{3,5},{4,6},{5,7},{6,0},{7,1},{8,10},{9,11},{10,... | collective-permute-start | bytes 786440 | tf_op jit(solution)/shard_map/ppermute | solution.py:132
  28.8 4.4 %collective-permute-start.3 = (bf16[64,2048]{1,0:T(8,128)(2,1)S(1)}, bf16[64,2048]{1,0:T(8,128)(2,1)S(1)}, u32[]{:S(2)}, u32[]{:S(2)}) collective-permute-start(bf16[64,2048]{1,0:T(8,128)(2,1)S(1)} %get-tuple-element.21), channel_id=1, source_target_pairs={{0,4},{1,5},{2,6},{3,7},{4,0},{5,1},{6,2},{7,3},{8,12},{9,13},{10,... | collective-permute-start | bytes 786440 | tf_op jit(solution)/shard_map/ppermute | solution.py:132
  33.1 3.1 %collective-permute-start.4 = (bf16[64,2048]{1,0:T(8,128)(2,1)S(1)}, bf16[64,2048]{1,0:T(8,128)(2,1)S(1)}, u32[]{:S(2)}, u32[]{:S(2)}) collective-permute-start(bf16[64,2048]{1,0:T(8,128)(2,1)S(1)} %get-tuple-element.22), channel_id=1, source_target_pairs={{0,6},{1,7},{2,0},{3,1},{4,2},{5,3},{6,4},{7,5},{8,14},{9,15},{10,... | collective-permute-start | bytes 786440 | tf_op jit(solution)/shard_map/ppermute | solution.py:132
  36.2 0.0 all-to-all-done
  36.3 0.7 %broadcast_in_dim.2 = bf16[16,40,128]{2,1,0:T(8,128)(2,1)} broadcast(bf16[40,128]{1,0:T(8,128)(2,1)S(1)} %pad_maximum_fusion), dimensions={1,2} | broadcast | bytes 174080 | tf_op jit(solution)/shard_map/broadcast_in_dim | solution.py:136
  37.0 11.6 %all-to-all-start.1 = ((bf16[64,5,2,128]{3,2,1,0:T(2,128)(2,1)}), bf16[64,5,2,128]{3,2,1,0:T(2,128)(2,1)S(1)}, u32[]{:S(2)}, u32[]{:S(2)}) async-start(bf16[64,5,2,128]{3,2,1,0:T(2,128)(2,1)} %bitcast.7), calls=%async_computation.1 | async-start | bytes 327680 | tf_op jit(solution)/shard_map/all_to_all | solution.py:138
  48.5 0.0 collective-permute-done.2
  48.6 0.0 collective-permute-done.4
  48.6 0.1 convert_add_fusion
  48.7 7.9 %collective-permute-start.5 = (bf16[32,2048]{1,0:T(8,128)(2,1)S(1)}, bf16[32,2048]{1,0:T(8,128)(2,1)S(1)}, u32[]{:S(2)}, u32[]{:S(2)}) collective-permute-start(bf16[32,2048]{1,0:T(8,128)(2,1)S(1)} %split.15), channel_id=1, source_target_pairs={{0,1},{1,0},{2,3},{3,2},{4,5},{5,4},{6,7},{7,6},{8,9},{9,8},{10,11... | collective-permute-start | bytes 393224 | tf_op jit(solution)/shard_map/ppermute | solution.py:144
  56.7 2.1 %all-to-all-done.1 = bf16[64,5,2,128]{3,2,1,0:T(2,128)(2,1)S(1)} async-done(((bf16[64,5,2,128]{3,2,1,0:T(2,128)(2,1)}), bf16[64,5,2,128]{3,2,1,0:T(2,128)(2,1)S(1)}, u32[]{:S(2)}, u32[]{:S(2)}) %all-to-all-start.1) | async-done | bytes 163872 | tf_op jit(solution)/shard_map/all_to_all | solution.py:138
  58.8 0.7 %convert_bitcast_fusion = f32[288,256]{1,0:T(8,128)} fusion(bf16[36,2,8,128]{3,2,1,0:T(8,128)(2,1)S(1)} %bitcast.23), kind=kLoop, calls=%fused_computation.2 | loop fusion | flops 73728 | bytes 442368 | tf_op jit(solution)/shard_map/convert_element_type | solution.py:145
  59.5 3.5 %collective-permute-done.5 = bf16[32,2048]{1,0:T(8,128)(2,1)S(1)} collective-permute-done((bf16[32,2048]{1,0:T(8,128)(2,1)S(1)}, bf16[32,2048]{1,0:T(8,128)(2,1)S(1)}, u32[]{:S(2)}, u32[]{:S(2)}) %collective-permute-start.5) | collective-permute-done | bytes 131104 | tf_op jit(solution)/shard_map/ppermute | solution.py:144
  63.0 0.7 %fusion = bf16[32,2048]{1,0:T(8,128)(2,1)} fusion(f32[64,2048]{1,0:T(8,128)S(1)} %convert_add_fusion, bf16[32,2048]{1,0:T(8,128)(2,1)S(1)} %collective-permute-done.5), kind=kLoop, calls=%fused_computation.5 | loop fusion | flops 196608 | bytes 524288 | tf_op jit(solution)/shard_map/convert_element_type | solution.py:147
  (12 shorter events, 0.1 us)
Async XLA Ops:
  0.6 0.9 %copy-start = (bf16[32,2048]{1,0:T(8,128)(2,1)S(1)}, bf16[32,2048]{1,0:T(8,128)(2,1)}, u32[]{:S(2)}) copy-start(bf16[32,2048]{1,0:T(8,128)(2,1)} %grad_ref.3) | copy-start | bytes 393220
  1.5 10.6 %copy-start.1 = (bf16[256,2048]{1,0:T(8,128)(2,1)S(1)}, bf16[256,2048]{1,0:T(8,128)(2,1)}, u32[]{:S(2)}) copy-start(bf16[256,2048]{1,0:T(8,128)(2,1)} %acts_ref.1) | copy-start | bytes 3145732
  1.6 9.8 %collective-permute-start = (bf16[32,1024]{1,0:T(8,128)(2,1)S(1)}, bf16[32,1024]{1,0:T(8,128)(2,1)S(1)}, u32[]{:S(2)}, u32[]{:S(2)}) collective-permute-start(bf16[32,1024]{1,0:T(8,128)(2,1)S(1)} %line.1), channel_id=1, source_target_pairs={{8,16},{24,32},{40,48},{56,64},{72,80},{88,96},{104,112},{120,128}... | collective-permute-start | bytes 196616 | tf_op jit(solution)/shard_map/ppermute | solution.py:23
  6.4 5.7 %collective-permute-start.1 = (bf16[32,1024]{1,0:T(8,128)(2,1)S(1)}, bf16[32,1024]{1,0:T(8,128)(2,1)S(1)}, u32[]{:S(2)}, u32[]{:S(2)}) collective-permute-start(bf16[32,1024]{1,0:T(8,128)(2,1)S(1)} %get-tuple-element.14), channel_id=1, source_target_pairs={{0,8},{8,0},{16,24},{24,16},{32,40},{40,32},{48,56},{56,48},{64,72... | collective-permute-start | bytes 196616 | tf_op jit(solution)/shard_map/ppermute | solution.py:23
  12.2 12.1 %copy-start.2 = (bf16[32,3,3,256]{3,0,2,1:T(8,128)(2,1)S(1)}, bf16[32,3,3,256]{3,0,2,1:T(8,128)(2,1)}, u32[]{:S(2)}) copy-start(bf16[32,3,3,256]{3,0,2,1:T(8,128)(2,1)} %param.5) | copy-start | bytes 442372
  13.4 22.8 %all-to-all-start = ((bf16[64,5,2,128]{3,2,1,0:T(2,128)(2,1)}), bf16[64,5,2,128]{3,2,1,0:T(2,128)(2,1)S(1)}, u32[]{:S(2)}, u32[]{:S(2)}) async-start(bf16[64,5,2,128]{3,2,1,0:T(2,128)(2,1)} %bitcast.5), calls=%async_computation | async-start | bytes 327680 | tf_op jit(solution)/shard_map/all_to_all | solution.py:115
  25.6 22.9 %collective-permute-start.2 = (bf16[64,2048]{1,0:T(8,128)(2,1)S(1)}, bf16[64,2048]{1,0:T(8,128)(2,1)S(1)}, u32[]{:S(2)}, u32[]{:S(2)}) collective-permute-start(bf16[64,2048]{1,0:T(8,128)(2,1)S(1)} %get-tuple-element.20), channel_id=1, source_target_pairs={{0,2},{1,3},{2,4},{3,5},{4,6},{5,7},{6,0},{7,1},{8,10},{9,11},{10,... | collective-permute-start | bytes 786440 | tf_op jit(solution)/shard_map/ppermute | solution.py:132
  28.8 19.8 %collective-permute-start.3 = (bf16[64,2048]{1,0:T(8,128)(2,1)S(1)}, bf16[64,2048]{1,0:T(8,128)(2,1)S(1)}, u32[]{:S(2)}, u32[]{:S(2)}) collective-permute-start(bf16[64,2048]{1,0:T(8,128)(2,1)S(1)} %get-tuple-element.21), channel_id=1, source_target_pairs={{0,4},{1,5},{2,6},{3,7},{4,0},{5,1},{6,2},{7,3},{8,12},{9,13},{10,... | collective-permute-start | bytes 786440 | tf_op jit(solution)/shard_map/ppermute | solution.py:132
  33.1 15.4 %collective-permute-start.4 = (bf16[64,2048]{1,0:T(8,128)(2,1)S(1)}, bf16[64,2048]{1,0:T(8,128)(2,1)S(1)}, u32[]{:S(2)}, u32[]{:S(2)}) collective-permute-start(bf16[64,2048]{1,0:T(8,128)(2,1)S(1)} %get-tuple-element.22), channel_id=1, source_target_pairs={{0,6},{1,7},{2,0},{3,1},{4,2},{5,3},{6,4},{7,5},{8,14},{9,15},{10,... | collective-permute-start | bytes 786440 | tf_op jit(solution)/shard_map/ppermute | solution.py:132
  37.0 21.8 %all-to-all-start.1 = ((bf16[64,5,2,128]{3,2,1,0:T(2,128)(2,1)}), bf16[64,5,2,128]{3,2,1,0:T(2,128)(2,1)S(1)}, u32[]{:S(2)}, u32[]{:S(2)}) async-start(bf16[64,5,2,128]{3,2,1,0:T(2,128)(2,1)} %bitcast.7), calls=%async_computation.1 | async-start | bytes 327680 | tf_op jit(solution)/shard_map/all_to_all | solution.py:138
  48.7 14.3 %collective-permute-start.5 = (bf16[32,2048]{1,0:T(8,128)(2,1)S(1)}, bf16[32,2048]{1,0:T(8,128)(2,1)S(1)}, u32[]{:S(2)}, u32[]{:S(2)}) collective-permute-start(bf16[32,2048]{1,0:T(8,128)(2,1)S(1)} %split.15), channel_id=1, source_target_pairs={{0,1},{1,0},{2,3},{3,2},{4,5},{5,4},{6,7},{7,6},{8,9},{9,8},{10,11... | collective-permute-start | bytes 393224 | tf_op jit(solution)/shard_map/ppermute | solution.py:144

commit v6 on v5

--- a/solution.py
+++ b/solution.py
@@ -112,7 +112,10 @@
         compiler_params=pltpu.CompilerParams(vmem_limit_bytes=32 << 20),
         name="outer",
     )(core, far, near, activations, inner)
-    got = lax.all_to_all(chunks.reshape(64, 5, 2, 128), "space", 0, 0, tiled=True).reshape(chunks.shape)
+    ring = [list(range(n_space // 4, n_space // 2)) + list(range(n_space // 4)) + list(range(n_space // 2, n_space))]
+    got = lax.all_to_all(
+        chunks.reshape(64, 5, 2, 128), "space", 0, 0, tiled=True, axis_index_groups=ring
+    ).reshape(chunks.shape)
 
     taps = kernel.transpose(1, 2, 0, 3).reshape(9 * filters, channels)
     part = jax.ShapeDtypeStruct((2 * share, pixels), jnp.bfloat16)
@@ -135,7 +138,9 @@
     total = ((four[0:10] + four[10:20]) + (four[20:30] + four[30:40])).astype(jnp.bfloat16)
     everyone = jnp.broadcast_to(jnp.concatenate([total] * 4, axis=0)[None], (16, 40, 128))
     own, everyone = lax.optimization_barrier((own, everyone))
-    full = lax.all_to_all(everyone.reshape(64, 5, 2, 128), "space", 0, 0, tiled=True).reshape(chunks.shape)
+    full = lax.all_to_all(
+        everyone.reshape(64, 5, 2, 128), "space", 0, 0, tiled=True, axis_index_groups=ring
+    ).reshape(chunks.shape)
 
     summed = own.astype(jnp.float32)
     for other in arrived:

time: 64.1 us -> 64 us (level)
  starting transfers between devices: 50.5 us -> 49.8 us
    ppermute x1, waiting for transfers between devices: 3.54 us -> 4.44 us  [body(): lax.ppermute(give.astype(jnp.bfloat16), 'filt', [(i, i ^ 1) for i in rang...]
    all_to_all x2, starting transfers between devices: 22.5 us -> 21.8 us  [the longest x1 11.1 us: body(): lax.all_to_all(chunks.reshape(64, 5, 2, 128), 'space', 0, 0, tiled=True,...]
where the time goes in v6:
time: 64 us; the launch traced here: 63.6 us
  starting transfers between devices  49.8 us (78%)
  waiting for transfers between devices  7.02 us (11%)
  Pallas kernels  2.68 us (4%)
  other arithmetic  1.67 us (3%)
  local copies, waits for them, and re-layouts  1.62 us (3%)
  between operations  0.83 us (1%)
    all_to_all x1, starting transfers between devices, body(): lax.all_to_all(chunks.reshape(64, 5, 2, 128), 'space', 0, 0, tiled=True,...  11.1 us
    all_to_all x1, starting transfers between devices, body(): lax.all_to_all(everyone.reshape(64, 5, 2, 128), 'space', 0, 0, tiled=True...  10.7 us
    ppermute x3, starting transfers between devices, body(): arrived.append(lax.ppermute(parts[k - 1], 'filt', pairs))  10.5 us
    ppermute x1, starting transfers between devices, body(): lax.ppermute(give.astype(jnp.bfloat16), 'filt', [(i, i ^ 1) for i in rang...  7.93 us
    ppermute x1, starting transfers between devices, halo_rows(): lax.ppermute(near, 'space', [(i, i ^ 1) for i in range(size)])  4.86 us
    ppermute x1, starting transfers between devices, halo_rows(): lax.ppermute(far, 'space', across)  4.72 us
    ppermute x1, waiting for transfers between devices, body(): lax.ppermute(give.astype(jnp.bfloat16), 'filt', [(i, i ^ 1) for i in rang...  4.44 us
    all_to_all x1, waiting for transfers between devices, body(): lax.all_to_all(everyone.reshape(64, 5, 2, 128), 'space', 0, 0, tiled=True...  1.78 us
  transfers between devices with their start and end apart: 8, of which 3 were waited for; matrix products, arithmetic and copies ran while one was open for 3% of the time, Pallas kernels for 2%

profile of v6, /device:TPU:1, one launch (start us, length us, event | category | flops | bytes accessed | tf_op | source)
XLA Modules:
  0.0 63.6 jit_solution(12101009780791062389)
XLA Ops:
  0.7 0.9 %copy-done = bf16[32,2048]{1,0:T(8,128)(2,1)S(1)} copy-done((bf16[32,2048]{1,0:T(8,128)(2,1)S(1)}, bf16[32,2048]{1,0:T(8,128)(2,1)}, u32[]{:S(2)}) %copy-start) | copy-done | bytes 131096
  1.6 4.7 %collective-permute-start = (bf16[32,1024]{1,0:T(8,128)(2,1)S(1)}, bf16[32,1024]{1,0:T(8,128)(2,1)S(1)}, u32[]{:S(2)}, u32[]{:S(2)}) collective-permute-start(bf16[32,1024]{1,0:T(8,128)(2,1)S(1)} %line.1), channel_id=1, source_target_pairs={{8,16},{24,32},{40,48},{56,64},{72,80},{88,96},{104,112},{120,128}... | collective-permute-start | bytes 196616 | tf_op jit(solution)/shard_map/ppermute | solution.py:23
  6.3 0.1 inner.1
  6.4 4.9 %collective-permute-start.1 = (bf16[32,1024]{1,0:T(8,128)(2,1)S(1)}, bf16[32,1024]{1,0:T(8,128)(2,1)S(1)}, u32[]{:S(2)}, u32[]{:S(2)}) collective-permute-start(bf16[32,1024]{1,0:T(8,128)(2,1)S(1)} %get-tuple-element.14), channel_id=1, source_target_pairs={{0,8},{8,0},{16,24},{24,16},{32,40},{40,32},{48,56},{56,48},{64,72... | collective-permute-start | bytes 196616 | tf_op jit(solution)/shard_map/ppermute | solution.py:23
  11.3 0.1 pad_add_fusion.where_ref
  11.4 0.0 collective-permute-done.far_ref
  11.4 0.8 %collective-permute-done.1.near_ref = bf16[32,1024]{1,0:T(8,128)(2,1)S(1)} collective-permute-done((bf16[32,1024]{1,0:T(8,128)(2,1)S(1)}, bf16[32,1024]{1,0:T(8,128)(2,1)S(1)}, u32[]{:S(2)}, u32[]{:S(2)}) %collective-permute-start.1) | collective-permute-done | bytes 65568 | tf_op jit(solution)/shard_map/ppermute | solution.py:23
  12.2 1.2 %outer.1 = (bf16[288,2048]{1,0:T(8,128)(2,1)S(1)}, bf16[80,8,128]{2,1,0:T(8,128)(2,1)}) custom-call(s32[1]{0:T(128)} %bitcast.4.core_ref, bf16[32,1024]{1,0:T(8,128)(2,1)S(1)} %collective-permute-done.far_ref, bf16[32,1024]{1,0:T(8,128)(2,1)S(1)} %collective-permute-done.1.near_ref, ...), custom_call_target="tpu_custom_call", output_to_operand_aliasing={{0}: (4, {})} | custom-call | flops 1000000000 | bytes 1048576 | tf_op jit(solution)/shard_map/outer/pallas_call | solution.py:107
  13.4 11.1 %all-to-all-start = ((bf16[64,5,2,128]{3,2,1,0:T(2,128)(2,1)}), bf16[64,5,2,128]{3,2,1,0:T(2,128)(2,1)S(1)}, u32[]{:S(2)}, u32[]{:S(2)}) async-start(bf16[64,5,2,128]{3,2,1,0:T(2,128)(2,1)} %bitcast.5), calls=%async_computation | async-start | bytes 327680 | tf_op jit(solution)/shard_map/all_to_all | solution.py:116
  24.5 1.3 %parts.1 = (bf16[64,2048]{1,0:T(8,128)(2,1)S(1)}, bf16[64,2048]{1,0:T(8,128)(2,1)S(1)}, bf16[64,2048]{1,0:T(8,128)(2,1)S(1)}, bf16[64,2048]{1,0:T(8,128)(2,1)S(1)}) custom-call(s32[2]{0:T(128)S(1)} %pad_add_fusion.where_ref, bf16[288,256]{1,0:T(8,128)(2,1)S(1)} %bitcast.20, bf16[288,2048]{1,0:T(8,128)(2,1)S(1)} %get-tuple-element.16.stack_ref), custom_call_target="tpu_custom_call" | custom-call | flops 115000000512 | bytes 1048576 | tf_op jit(solution)/shard_map/parts/pallas_call | solution.py:122
  25.9 3.1 %collective-permute-start.2 = (bf16[64,2048]{1,0:T(8,128)(2,1)S(1)}, bf16[64,2048]{1,0:T(8,128)(2,1)S(1)}, u32[]{:S(2)}, u32[]{:S(2)}) collective-permute-start(bf16[64,2048]{1,0:T(8,128)(2,1)S(1)} %get-tuple-element.20), channel_id=1, source_target_pairs={{0,2},{1,3},{2,4},{3,5},{4,6},{5,7},{6,0},{7,1},{8,10},{9,11},{10,... | collective-permute-start | bytes 786440 | tf_op jit(solution)/shard_map/ppermute | solution.py:135
  29.0 4.4 %collective-permute-start.3 = (bf16[64,2048]{1,0:T(8,128)(2,1)S(1)}, bf16[64,2048]{1,0:T(8,128)(2,1)S(1)}, u32[]{:S(2)}, u32[]{:S(2)}) collective-permute-start(bf16[64,2048]{1,0:T(8,128)(2,1)S(1)} %get-tuple-element.21), channel_id=1, source_target_pairs={{0,4},{1,5},{2,6},{3,7},{4,0},{5,1},{6,2},{7,3},{8,12},{9,13},{10,... | collective-permute-start | bytes 786440 | tf_op jit(solution)/shard_map/ppermute | solution.py:135
  33.3 3.1 %collective-permute-start.4 = (bf16[64,2048]{1,0:T(8,128)(2,1)S(1)}, bf16[64,2048]{1,0:T(8,128)(2,1)S(1)}, u32[]{:S(2)}, u32[]{:S(2)}) collective-permute-start(bf16[64,2048]{1,0:T(8,128)(2,1)S(1)} %get-tuple-element.22), channel_id=1, source_target_pairs={{0,6},{1,7},{2,0},{3,1},{4,2},{5,3},{6,4},{7,5},{8,14},{9,15},{10,... | collective-permute-start | bytes 786440 | tf_op jit(solution)/shard_map/ppermute | solution.py:135
  36.4 0.0 all-to-all-done
  36.5 0.7 %broadcast_in_dim.2 = bf16[16,40,128]{2,1,0:T(8,128)(2,1)} broadcast(bf16[40,128]{1,0:T(8,128)(2,1)S(1)} %pad_maximum_fusion), dimensions={1,2} | broadcast | bytes 174080 | tf_op jit(solution)/shard_map/broadcast_in_dim | solution.py:139
  37.2 10.7 %all-to-all-start.1 = ((bf16[64,5,2,128]{3,2,1,0:T(2,128)(2,1)}), bf16[64,5,2,128]{3,2,1,0:T(2,128)(2,1)S(1)}, u32[]{:S(2)}, u32[]{:S(2)}) async-start(bf16[64,5,2,128]{3,2,1,0:T(2,128)(2,1)} %bitcast.7), calls=%async_computation.1 | async-start | bytes 327680 | tf_op jit(solution)/shard_map/all_to_all | solution.py:141
  47.9 0.0 collective-permute-done.2
  47.9 0.0 collective-permute-done.4
  47.9 0.1 convert_add_fusion
  48.0 7.9 %collective-permute-start.5 = (bf16[32,2048]{1,0:T(8,128)(2,1)S(1)}, bf16[32,2048]{1,0:T(8,128)(2,1)S(1)}, u32[]{:S(2)}, u32[]{:S(2)}) collective-permute-start(bf16[32,2048]{1,0:T(8,128)(2,1)S(1)} %split.15), channel_id=1, source_target_pairs={{0,1},{1,0},{2,3},{3,2},{4,5},{5,4},{6,7},{7,6},{8,9},{9,8},{10,11... | collective-permute-start | bytes 393224 | tf_op jit(solution)/shard_map/ppermute | solution.py:149
  56.0 1.8 %all-to-all-done.1 = bf16[64,5,2,128]{3,2,1,0:T(2,128)(2,1)S(1)} async-done(((bf16[64,5,2,128]{3,2,1,0:T(2,128)(2,1)}), bf16[64,5,2,128]{3,2,1,0:T(2,128)(2,1)S(1)}, u32[]{:S(2)}, u32[]{:S(2)}) %all-to-all-start.1) | async-done | bytes 163872 | tf_op jit(solution)/shard_map/all_to_all | solution.py:141
  57.8 0.7 %convert_bitcast_fusion = f32[288,256]{1,0:T(8,128)} fusion(bf16[36,2,8,128]{3,2,1,0:T(8,128)(2,1)S(1)} %bitcast.23), kind=kLoop, calls=%fused_computation.2 | loop fusion | flops 73728 | bytes 442368 | tf_op jit(solution)/shard_map/convert_element_type | solution.py:150
  58.5 4.4 %collective-permute-done.5 = bf16[32,2048]{1,0:T(8,128)(2,1)S(1)} collective-permute-done((bf16[32,2048]{1,0:T(8,128)(2,1)S(1)}, bf16[32,2048]{1,0:T(8,128)(2,1)S(1)}, u32[]{:S(2)}, u32[]{:S(2)}) %collective-permute-start.5) | collective-permute-done | bytes 131104 | tf_op jit(solution)/shard_map/ppermute | solution.py:149
  63.0 0.7 %fusion = bf16[32,2048]{1,0:T(8,128)(2,1)} fusion(f32[64,2048]{1,0:T(8,128)S(1)} %convert_add_fusion, bf16[32,2048]{1,0:T(8,128)(2,1)S(1)} %collective-permute-done.5), kind=kLoop, calls=%fused_computation.5 | loop fusion | flops 196608 | bytes 524288 | tf_op jit(solution)/shard_map/convert_element_type | solution.py:152
  (12 shorter events, 0.1 us)
Async XLA Ops:
  0.6 0.9 %copy-start = (bf16[32,2048]{1,0:T(8,128)(2,1)S(1)}, bf16[32,2048]{1,0:T(8,128)(2,1)}, u32[]{:S(2)}) copy-start(bf16[32,2048]{1,0:T(8,128)(2,1)} %grad_ref.3) | copy-start | bytes 393220
  1.5 10.6 %copy-start.1 = (bf16[256,2048]{1,0:T(8,128)(2,1)S(1)}, bf16[256,2048]{1,0:T(8,128)(2,1)}, u32[]{:S(2)}) copy-start(bf16[256,2048]{1,0:T(8,128)(2,1)} %acts_ref.1) | copy-start | bytes 3145732
  1.6 9.8 %collective-permute-start = (bf16[32,1024]{1,0:T(8,128)(2,1)S(1)}, bf16[32,1024]{1,0:T(8,128)(2,1)S(1)}, u32[]{:S(2)}, u32[]{:S(2)}) collective-permute-start(bf16[32,1024]{1,0:T(8,128)(2,1)S(1)} %line.1), channel_id=1, source_target_pairs={{8,16},{24,32},{40,48},{56,64},{72,80},{88,96},{104,112},{120,128}... | collective-permute-start | bytes 196616 | tf_op jit(solution)/shard_map/ppermute | solution.py:23
  6.4 5.7 %collective-permute-start.1 = (bf16[32,1024]{1,0:T(8,128)(2,1)S(1)}, bf16[32,1024]{1,0:T(8,128)(2,1)S(1)}, u32[]{:S(2)}, u32[]{:S(2)}) collective-permute-start(bf16[32,1024]{1,0:T(8,128)(2,1)S(1)} %get-tuple-element.14), channel_id=1, source_target_pairs={{0,8},{8,0},{16,24},{24,16},{32,40},{40,32},{48,56},{56,48},{64,72... | collective-permute-start | bytes 196616 | tf_op jit(solution)/shard_map/ppermute | solution.py:23
  12.2 12.3 %copy-start.2 = (bf16[32,3,3,256]{3,0,2,1:T(8,128)(2,1)S(1)}, bf16[32,3,3,256]{3,0,2,1:T(8,128)(2,1)}, u32[]{:S(2)}) copy-start(bf16[32,3,3,256]{3,0,2,1:T(8,128)(2,1)} %param.5) | copy-start | bytes 442372
  13.4 23.0 %all-to-all-start = ((bf16[64,5,2,128]{3,2,1,0:T(2,128)(2,1)}), bf16[64,5,2,128]{3,2,1,0:T(2,128)(2,1)S(1)}, u32[]{:S(2)}, u32[]{:S(2)}) async-start(bf16[64,5,2,128]{3,2,1,0:T(2,128)(2,1)} %bitcast.5), calls=%async_computation | async-start | bytes 327680 | tf_op jit(solution)/shard_map/all_to_all | solution.py:116
  25.9 22.0 %collective-permute-start.2 = (bf16[64,2048]{1,0:T(8,128)(2,1)S(1)}, bf16[64,2048]{1,0:T(8,128)(2,1)S(1)}, u32[]{:S(2)}, u32[]{:S(2)}) collective-permute-start(bf16[64,2048]{1,0:T(8,128)(2,1)S(1)} %get-tuple-element.20), channel_id=1, source_target_pairs={{0,2},{1,3},{2,4},{3,5},{4,6},{5,7},{6,0},{7,1},{8,10},{9,11},{10,... | collective-permute-start | bytes 786440 | tf_op jit(solution)/shard_map/ppermute | solution.py:135
  29.0 18.9 %collective-permute-start.3 = (bf16[64,2048]{1,0:T(8,128)(2,1)S(1)}, bf16[64,2048]{1,0:T(8,128)(2,1)S(1)}, u32[]{:S(2)}, u32[]{:S(2)}) collective-permute-start(bf16[64,2048]{1,0:T(8,128)(2,1)S(1)} %get-tuple-element.21), channel_id=1, source_target_pairs={{0,4},{1,5},{2,6},{3,7},{4,0},{5,1},{6,2},{7,3},{8,12},{9,13},{10,... | collective-permute-start | bytes 786440 | tf_op jit(solution)/shard_map/ppermute | solution.py:135
  33.3 14.5 %collective-permute-start.4 = (bf16[64,2048]{1,0:T(8,128)(2,1)S(1)}, bf16[64,2048]{1,0:T(8,128)(2,1)S(1)}, u32[]{:S(2)}, u32[]{:S(2)}) collective-permute-start(bf16[64,2048]{1,0:T(8,128)(2,1)S(1)} %get-tuple-element.22), channel_id=1, source_target_pairs={{0,6},{1,7},{2,0},{3,1},{4,2},{5,3},{6,4},{7,5},{8,14},{9,15},{10,... | collective-permute-start | bytes 786440 | tf_op jit(solution)/shard_map/ppermute | solution.py:135
  37.2 20.6 %all-to-all-start.1 = ((bf16[64,5,2,128]{3,2,1,0:T(2,128)(2,1)}), bf16[64,5,2,128]{3,2,1,0:T(2,128)(2,1)S(1)}, u32[]{:S(2)}, u32[]{:S(2)}) async-start(bf16[64,5,2,128]{3,2,1,0:T(2,128)(2,1)} %bitcast.7), calls=%async_computation.1 | async-start | bytes 327680 | tf_op jit(solution)/shard_map/all_to_all | solution.py:141
  48.0 14.9 %collective-permute-start.5 = (bf16[32,2048]{1,0:T(8,128)(2,1)S(1)}, bf16[32,2048]{1,0:T(8,128)(2,1)S(1)}, u32[]{:S(2)}, u32[]{:S(2)}) collective-permute-start(bf16[32,2048]{1,0:T(8,128)(2,1)S(1)} %split.15), channel_id=1, source_target_pairs={{0,1},{1,0},{2,3},{3,2},{4,5},{5,4},{6,7},{7,6},{8,9},{9,8},{10,11... | collective-permute-start | bytes 393224 | tf_op jit(solution)/shard_map/ppermute | solution.py:149

commit v7 on v6

--- a/solution.py
+++ b/solution.py
@@ -112,7 +112,8 @@
         compiler_params=pltpu.CompilerParams(vmem_limit_bytes=32 << 20),
         name="outer",
     )(core, far, near, activations, inner)
-    ring = [list(range(n_space // 4, n_space // 2)) + list(range(n_space // 4)) + list(range(n_space // 2, n_space))]
+    middle = n_space // 2
+    ring = [list(range(middle, n_space)) + list(range(middle))]
     got = lax.all_to_all(
         chunks.reshape(64, 5, 2, 128), "space", 0, 0, tiled=True, axis_index_groups=ring
     ).reshape(chunks.shape)

time: 64 us -> 65.6 us (1.025)
  waiting for transfers between devices: 7.02 us -> 8.57 us
    ppermute x1, waiting for transfers between devices: 4.44 us -> 6.42 us  [body(): lax.ppermute(give.astype(jnp.bfloat16), 'filt', [(i, i ^ 1) for i in rang...]
where the time goes in v7:
time: 65.6 us; the launch traced here: 65.2 us
  starting transfers between devices  49.8 us (76%)
  waiting for transfers between devices  8.57 us (13%)
  Pallas kernels  2.68 us (4%)
  other arithmetic  1.67 us (3%)
  local copies, waits for them, and re-layouts  1.62 us (2%)
  between operations  0.83 us (1%)
    all_to_all x1, starting transfers between devices, body(): lax.all_to_all(chunks.reshape(64, 5, 2, 128), 'space', 0, 0, tiled=True,...  11.2 us
    all_to_all x1, starting transfers between devices, body(): lax.all_to_all(everyone.reshape(64, 5, 2, 128), 'space', 0, 0, tiled=True...  10.6 us
    ppermute x3, starting transfers between devices, body(): arrived.append(lax.ppermute(parts[k - 1], 'filt', pairs))  10.5 us
    ppermute x1, starting transfers between devices, body(): lax.ppermute(give.astype(jnp.bfloat16), 'filt', [(i, i ^ 1) for i in rang...  7.94 us
    ppermute x1, waiting for transfers between devices, body(): lax.ppermute(give.astype(jnp.bfloat16), 'filt', [(i, i ^ 1) for i in rang...  6.42 us
    ppermute x1, starting transfers between devices, halo_rows(): lax.ppermute(near, 'space', [(i, i ^ 1) for i in range(size)])  4.86 us
    ppermute x1, starting transfers between devices, halo_rows(): lax.ppermute(far, 'space', across)  4.72 us
    all_to_all x1, waiting for transfers between devices, body(): lax.all_to_all(everyone.reshape(64, 5, 2, 128), 'space', 0, 0, tiled=True...  1.36 us
  transfers between devices with their start and end apart: 8, of which 3 were waited for; matrix products, arithmetic and copies ran while one was open for 3% of the time, Pallas kernels for 2%

profile of v7, /device:TPU:1, one launch (start us, length us, event | category | flops | bytes accessed | tf_op | source)
XLA Modules:
  0.0 65.2 jit_solution(11304010758380317851)
XLA Ops:
  0.7 0.9 %copy-done = bf16[32,2048]{1,0:T(8,128)(2,1)S(1)} copy-done((bf16[32,2048]{1,0:T(8,128)(2,1)S(1)}, bf16[32,2048]{1,0:T(8,128)(2,1)}, u32[]{:S(2)}) %copy-start) | copy-done | bytes 131096
  1.6 4.7 %collective-permute-start = (bf16[32,1024]{1,0:T(8,128)(2,1)S(1)}, bf16[32,1024]{1,0:T(8,128)(2,1)S(1)}, u32[]{:S(2)}, u32[]{:S(2)}) collective-permute-start(bf16[32,1024]{1,0:T(8,128)(2,1)S(1)} %line.1), channel_id=1, source_target_pairs={{8,16},{24,32},{40,48},{56,64},{72,80},{88,96},{104,112},{120,128}... | collective-permute-start | bytes 196616 | tf_op jit(solution)/shard_map/ppermute | solution.py:23
  6.3 0.1 inner.1
  6.4 4.9 %collective-permute-start.1 = (bf16[32,1024]{1,0:T(8,128)(2,1)S(1)}, bf16[32,1024]{1,0:T(8,128)(2,1)S(1)}, u32[]{:S(2)}, u32[]{:S(2)}) collective-permute-start(bf16[32,1024]{1,0:T(8,128)(2,1)S(1)} %get-tuple-element.14), channel_id=1, source_target_pairs={{0,8},{8,0},{16,24},{24,16},{32,40},{40,32},{48,56},{56,48},{64,72... | collective-permute-start | bytes 196616 | tf_op jit(solution)/shard_map/ppermute | solution.py:23
  11.3 0.1 pad_add_fusion.where_ref
  11.4 0.0 collective-permute-done.far_ref
  11.4 0.8 %collective-permute-done.1.near_ref = bf16[32,1024]{1,0:T(8,128)(2,1)S(1)} collective-permute-done((bf16[32,1024]{1,0:T(8,128)(2,1)S(1)}, bf16[32,1024]{1,0:T(8,128)(2,1)S(1)}, u32[]{:S(2)}, u32[]{:S(2)}) %collective-permute-start.1) | collective-permute-done | bytes 65568 | tf_op jit(solution)/shard_map/ppermute | solution.py:23
  12.2 1.2 %outer.1 = (bf16[288,2048]{1,0:T(8,128)(2,1)S(1)}, bf16[80,8,128]{2,1,0:T(8,128)(2,1)}) custom-call(s32[1]{0:T(128)} %bitcast.4.core_ref, bf16[32,1024]{1,0:T(8,128)(2,1)S(1)} %collective-permute-done.far_ref, bf16[32,1024]{1,0:T(8,128)(2,1)S(1)} %collective-permute-done.1.near_ref, ...), custom_call_target="tpu_custom_call", output_to_operand_aliasing={{0}: (4, {})} | custom-call | flops 1000000000 | bytes 1048576 | tf_op jit(solution)/shard_map/outer/pallas_call | solution.py:107
  13.4 11.2 %all-to-all-start = ((bf16[64,5,2,128]{3,2,1,0:T(2,128)(2,1)}), bf16[64,5,2,128]{3,2,1,0:T(2,128)(2,1)S(1)}, u32[]{:S(2)}, u32[]{:S(2)}) async-start(bf16[64,5,2,128]{3,2,1,0:T(2,128)(2,1)} %bitcast.5), calls=%async_computation | async-start | bytes 327680 | tf_op jit(solution)/shard_map/all_to_all | solution.py:117
  24.6 1.3 %parts.1 = (bf16[64,2048]{1,0:T(8,128)(2,1)S(1)}, bf16[64,2048]{1,0:T(8,128)(2,1)S(1)}, bf16[64,2048]{1,0:T(8,128)(2,1)S(1)}, bf16[64,2048]{1,0:T(8,128)(2,1)S(1)}) custom-call(s32[2]{0:T(128)S(1)} %pad_add_fusion.where_ref, bf16[288,256]{1,0:T(8,128)(2,1)S(1)} %bitcast.20, bf16[288,2048]{1,0:T(8,128)(2,1)S(1)} %get-tuple-element.16.stack_ref), custom_call_target="tpu_custom_call" | custom-call | flops 115000000512 | bytes 1048576 | tf_op jit(solution)/shard_map/parts/pallas_call | solution.py:123
  25.9 3.1 %collective-permute-start.2 = (bf16[64,2048]{1,0:T(8,128)(2,1)S(1)}, bf16[64,2048]{1,0:T(8,128)(2,1)S(1)}, u32[]{:S(2)}, u32[]{:S(2)}) collective-permute-start(bf16[64,2048]{1,0:T(8,128)(2,1)S(1)} %get-tuple-element.20), channel_id=1, source_target_pairs={{0,2},{1,3},{2,4},{3,5},{4,6},{5,7},{6,0},{7,1},{8,10},{9,11},{10,... | collective-permute-start | bytes 786440 | tf_op jit(solution)/shard_map/ppermute | solution.py:136
  29.1 4.4 %collective-permute-start.3 = (bf16[64,2048]{1,0:T(8,128)(2,1)S(1)}, bf16[64,2048]{1,0:T(8,128)(2,1)S(1)}, u32[]{:S(2)}, u32[]{:S(2)}) collective-permute-start(bf16[64,2048]{1,0:T(8,128)(2,1)S(1)} %get-tuple-element.21), channel_id=1, source_target_pairs={{0,4},{1,5},{2,6},{3,7},{4,0},{5,1},{6,2},{7,3},{8,12},{9,13},{10,... | collective-permute-start | bytes 786440 | tf_op jit(solution)/shard_map/ppermute | solution.py:136
  33.4 3.1 %collective-permute-start.4 = (bf16[64,2048]{1,0:T(8,128)(2,1)S(1)}, bf16[64,2048]{1,0:T(8,128)(2,1)S(1)}, u32[]{:S(2)}, u32[]{:S(2)}) collective-permute-start(bf16[64,2048]{1,0:T(8,128)(2,1)S(1)} %get-tuple-element.22), channel_id=1, source_target_pairs={{0,6},{1,7},{2,0},{3,1},{4,2},{5,3},{6,4},{7,5},{8,14},{9,15},{10,... | collective-permute-start | bytes 786440 | tf_op jit(solution)/shard_map/ppermute | solution.py:136
  36.5 0.0 all-to-all-done
  36.6 0.7 %broadcast_in_dim.2 = bf16[16,40,128]{2,1,0:T(8,128)(2,1)} broadcast(bf16[40,128]{1,0:T(8,128)(2,1)S(1)} %pad_maximum_fusion), dimensions={1,2} | broadcast | bytes 174080 | tf_op jit(solution)/shard_map/broadcast_in_dim | solution.py:140
  37.3 10.6 %all-to-all-start.1 = ((bf16[64,5,2,128]{3,2,1,0:T(2,128)(2,1)}), bf16[64,5,2,128]{3,2,1,0:T(2,128)(2,1)S(1)}, u32[]{:S(2)}, u32[]{:S(2)}) async-start(bf16[64,5,2,128]{3,2,1,0:T(2,128)(2,1)} %bitcast.7), calls=%async_computation.1 | async-start | bytes 327680 | tf_op jit(solution)/shard_map/all_to_all | solution.py:142
  47.8 0.0 collective-permute-done.2
  47.9 0.0 collective-permute-done.4
  47.9 0.1 convert_add_fusion
  48.0 7.9 %collective-permute-start.5 = (bf16[32,2048]{1,0:T(8,128)(2,1)S(1)}, bf16[32,2048]{1,0:T(8,128)(2,1)S(1)}, u32[]{:S(2)}, u32[]{:S(2)}) collective-permute-start(bf16[32,2048]{1,0:T(8,128)(2,1)S(1)} %split.15), channel_id=1, source_target_pairs={{0,1},{1,0},{2,3},{3,2},{4,5},{5,4},{6,7},{7,6},{8,9},{9,8},{10,11... | collective-permute-start | bytes 393224 | tf_op jit(solution)/shard_map/ppermute | solution.py:150
  56.0 1.4 %all-to-all-done.1 = bf16[64,5,2,128]{3,2,1,0:T(2,128)(2,1)S(1)} async-done(((bf16[64,5,2,128]{3,2,1,0:T(2,128)(2,1)}), bf16[64,5,2,128]{3,2,1,0:T(2,128)(2,1)S(1)}, u32[]{:S(2)}, u32[]{:S(2)}) %all-to-all-start.1) | async-done | bytes 163872 | tf_op jit(solution)/shard_map/all_to_all | solution.py:142
  57.3 0.7 %convert_bitcast_fusion = f32[288,256]{1,0:T(8,128)} fusion(bf16[36,2,8,128]{3,2,1,0:T(8,128)(2,1)S(1)} %bitcast.23), kind=kLoop, calls=%fused_computation.2 | loop fusion | flops 73728 | bytes 442368 | tf_op jit(solution)/shard_map/convert_element_type | solution.py:151
  58.1 6.4 %collective-permute-done.5 = bf16[32,2048]{1,0:T(8,128)(2,1)S(1)} collective-permute-done((bf16[32,2048]{1,0:T(8,128)(2,1)S(1)}, bf16[32,2048]{1,0:T(8,128)(2,1)S(1)}, u32[]{:S(2)}, u32[]{:S(2)}) %collective-permute-start.5) | collective-permute-done | bytes 131104 | tf_op jit(solution)/shard_map/ppermute | solution.py:150
  64.5 0.7 %fusion = bf16[32,2048]{1,0:T(8,128)(2,1)} fusion(f32[64,2048]{1,0:T(8,128)S(1)} %convert_add_fusion, bf16[32,2048]{1,0:T(8,128)(2,1)S(1)} %collective-permute-done.5), kind=kLoop, calls=%fused_computation.5 | loop fusion | flops 196608 | bytes 524288 | tf_op jit(solution)/shard_map/convert_element_type | solution.py:153
  (12 shorter events, 0.1 us)
Async XLA Ops:
  0.6 0.9 %copy-start = (bf16[32,2048]{1,0:T(8,128)(2,1)S(1)}, bf16[32,2048]{1,0:T(8,128)(2,1)}, u32[]{:S(2)}) copy-start(bf16[32,2048]{1,0:T(8,128)(2,1)} %grad_ref.3) | copy-start | bytes 393220
  1.5 10.6 %copy-start.1 = (bf16[256,2048]{1,0:T(8,128)(2,1)S(1)}, bf16[256,2048]{1,0:T(8,128)(2,1)}, u32[]{:S(2)}) copy-start(bf16[256,2048]{1,0:T(8,128)(2,1)} %acts_ref.1) | copy-start | bytes 3145732
  1.6 9.8 %collective-permute-start = (bf16[32,1024]{1,0:T(8,128)(2,1)S(1)}, bf16[32,1024]{1,0:T(8,128)(2,1)S(1)}, u32[]{:S(2)}, u32[]{:S(2)}) collective-permute-start(bf16[32,1024]{1,0:T(8,128)(2,1)S(1)} %line.1), channel_id=1, source_target_pairs={{8,16},{24,32},{40,48},{56,64},{72,80},{88,96},{104,112},{120,128}... | collective-permute-start | bytes 196616 | tf_op jit(solution)/shard_map/ppermute | solution.py:23
  6.4 5.7 %collective-permute-start.1 = (bf16[32,1024]{1,0:T(8,128)(2,1)S(1)}, bf16[32,1024]{1,0:T(8,128)(2,1)S(1)}, u32[]{:S(2)}, u32[]{:S(2)}) collective-permute-start(bf16[32,1024]{1,0:T(8,128)(2,1)S(1)} %get-tuple-element.14), channel_id=1, source_target_pairs={{0,8},{8,0},{16,24},{24,16},{32,40},{40,32},{48,56},{56,48},{64,72... | collective-permute-start | bytes 196616 | tf_op jit(solution)/shard_map/ppermute | solution.py:23
  12.2 12.4 %copy-start.2 = (bf16[32,3,3,256]{3,0,2,1:T(8,128)(2,1)S(1)}, bf16[32,3,3,256]{3,0,2,1:T(8,128)(2,1)}, u32[]{:S(2)}) copy-start(bf16[32,3,3,256]{3,0,2,1:T(8,128)(2,1)} %param.5) | copy-start | bytes 442372
  13.4 23.1 %all-to-all-start = ((bf16[64,5,2,128]{3,2,1,0:T(2,128)(2,1)}), bf16[64,5,2,128]{3,2,1,0:T(2,128)(2,1)S(1)}, u32[]{:S(2)}, u32[]{:S(2)}) async-start(bf16[64,5,2,128]{3,2,1,0:T(2,128)(2,1)} %bitcast.5), calls=%async_computation | async-start | bytes 327680 | tf_op jit(solution)/shard_map/all_to_all | solution.py:117
  25.9 21.9 %collective-permute-start.2 = (bf16[64,2048]{1,0:T(8,128)(2,1)S(1)}, bf16[64,2048]{1,0:T(8,128)(2,1)S(1)}, u32[]{:S(2)}, u32[]{:S(2)}) collective-permute-start(bf16[64,2048]{1,0:T(8,128)(2,1)S(1)} %get-tuple-element.20), channel_id=1, source_target_pairs={{0,2},{1,3},{2,4},{3,5},{4,6},{5,7},{6,0},{7,1},{8,10},{9,11},{10,... | collective-permute-start | bytes 786440 | tf_op jit(solution)/shard_map/ppermute | solution.py:136
  29.1 18.8 %collective-permute-start.3 = (bf16[64,2048]{1,0:T(8,128)(2,1)S(1)}, bf16[64,2048]{1,0:T(8,128)(2,1)S(1)}, u32[]{:S(2)}, u32[]{:S(2)}) collective-permute-start(bf16[64,2048]{1,0:T(8,128)(2,1)S(1)} %get-tuple-element.21), channel_id=1, source_target_pairs={{0,4},{1,5},{2,6},{3,7},{4,0},{5,1},{6,2},{7,3},{8,12},{9,13},{10,... | collective-permute-start | bytes 786440 | tf_op jit(solution)/shard_map/ppermute | solution.py:136
  33.4 14.4 %collective-permute-start.4 = (bf16[64,2048]{1,0:T(8,128)(2,1)S(1)}, bf16[64,2048]{1,0:T(8,128)(2,1)S(1)}, u32[]{:S(2)}, u32[]{:S(2)}) collective-permute-start(bf16[64,2048]{1,0:T(8,128)(2,1)S(1)} %get-tuple-element.22), channel_id=1, source_target_pairs={{0,6},{1,7},{2,0},{3,1},{4,2},{5,3},{6,4},{7,5},{8,14},{9,15},{10,... | collective-permute-start | bytes 786440 | tf_op jit(solution)/shard_map/ppermute | solution.py:136
  37.3 20.1 %all-to-all-start.1 = ((bf16[64,5,2,128]{3,2,1,0:T(2,128)(2,1)}), bf16[64,5,2,128]{3,2,1,0:T(2,128)(2,1)S(1)}, u32[]{:S(2)}, u32[]{:S(2)}) async-start(bf16[64,5,2,128]{3,2,1,0:T(2,128)(2,1)} %bitcast.7), calls=%async_computation.1 | async-start | bytes 327680 | tf_op jit(solution)/shard_map/all_to_all | solution.py:142
  48.0 16.5 %collective-permute-start.5 = (bf16[32,2048]{1,0:T(8,128)(2,1)S(1)}, bf16[32,2048]{1,0:T(8,128)(2,1)S(1)}, u32[]{:S(2)}, u32[]{:S(2)}) collective-permute-start(bf16[32,2048]{1,0:T(8,128)(2,1)S(1)} %split.15), channel_id=1, source_target_pairs={{0,1},{1,0},{2,3},{3,2},{4,5},{5,4},{6,7},{7,6},{8,9},{9,8},{10,11... | collective-permute-start | bytes 393224 | tf_op jit(solution)/shard_map/ppermute | solution.py:150
